TPU v7x, 512 devices: a whole 4x4x16 slice. The times are simulated.
512 devices in a mesh: dp: 16 (over y, x_hi, core), blk: 32 (over x_lo, z).
Axes of the slice: x: 4 (x_hi: 2, x_lo: 2; x = x_hi * 2 + x_lo), y: 4, z: 16, core: 2. Of those that a mesh axis runs over, the one named last changes fastest.
Arguments:
- pre_gelu: bfloat16 [98304, 4096], P(('dp', 'blk')), may hold values from -8 to 8
- out_grad: bfloat16 [98304, 1024], P(('dp', 'blk')), may hold values from -6 to 6
- down_weight: bfloat16 [4096, 1024], P('blk'), may hold values from -0.09375 to 0.09375
Outputs:
- block_out: bfloat16 [98304, 1024], P(('dp', 'blk'))
- pre_grad: bfloat16 [98304, 4096], P(('dp', 'blk'))
- weight_grad: float32 [4096, 1024], P('blk')
All inputs are finite; a program needn't handle non-finite values.
Results may differ from a plain program's by a relative error of at most 0.017.
Values may be sent and summed in bfloat16 or wider, within the bound.
A program may use at most 64 MiB of HBM per device.

v0:
```python
import math

import jax
import jax.numpy as jnp
from jax import lax
from jax.sharding import PartitionSpec as P

SQRT_TWO_PI = 0.7978845608028654
CUBIC = 0.044715


def passed_along(array, axis, by):
    peers = lax.axis_size(axis)
    return lax.ppermute(array, axis, [(i, (i + by) % peers) for i in range(peers)])


def gelu_parts(inputs):
    argument = SQRT_TWO_PI * (inputs + CUBIC * inputs * inputs * inputs)
    tangent = jnp.tanh(argument)
    activation = 0.5 * inputs * (1.0 + tangent)
    derivative = 0.5 * (1.0 + tangent) + 0.5 * inputs * (1.0 - tangent * tangent) * SQRT_TWO_PI * (
        1.0 + 3.0 * CUBIC * inputs * inputs
    )
    return (activation, derivative)


def finish_partial(arrived, own_term):
    rounded = (arrived.astype(jnp.float32) + own_term).astype(jnp.bfloat16)
    return lax.optimization_barrier(rounded).astype(jnp.float32)


def body(pre_gelu, out_grad, down_weight):
    row_count = pre_gelu.shape[0]
    model_width = out_grad.shape[1]
    block_rows = down_weight.shape[0]
    cycle_size = lax.axis_size("blk")
    home_index = lax.axis_index("blk")
    activation, derivative = gelu_parts(pre_gelu.astype(jnp.float32))
    hidden = activation.astype(jnp.bfloat16)

    def visit(weight, column, carried):
        out_total, grad_buffer = carried
        part_width = weight.shape[0]
        hidden_part = lax.dynamic_slice_in_dim(hidden, column, part_width, 1)
        slope_part = lax.dynamic_slice_in_dim(derivative, column, part_width, 1)
        out_total = out_total + jnp.dot(hidden_part, weight, preferred_element_type=jnp.float32)
        d_hidden = lax.dot_general(
            out_grad, weight, (((1,), (1,)), ((), ())), preferred_element_type=jnp.float32
        )
        grad_buffer = lax.dynamic_update_slice_in_dim(
            grad_buffer, (d_hidden * slope_part).astype(jnp.bfloat16), column, 1
        )
        contribution = lax.dot_general(
            hidden_part, out_grad, (((0,), (0,)), ((), ())), preferred_element_type=jnp.float32
        )
        return ((out_total, grad_buffer), contribution)

    carried = (
        jnp.zeros((row_count, model_width), jnp.float32),
        jnp.zeros(pre_gelu.shape, jnp.bfloat16),
    )

    def pass_weight(weight):
        return passed_along(weight, "blk", 1)

    def pass_grad(partial_value):
        return passed_along(partial_value, "blk", 1)

    carried, own_term = visit(down_weight, home_index * block_rows, carried)
    weight = pass_weight(down_weight)
    carried, contribution = visit(weight, jnp.mod(home_index - 1, cycle_size) * block_rows, carried)
    partial_value = contribution.astype(jnp.bfloat16)

    def one_stop(stop_number, loop_state):
        weight, partial_value, carried = loop_state
        weight = pass_weight(weight)
        carried, contribution = visit(
            weight, jnp.mod(home_index - stop_number, cycle_size) * block_rows, carried
        )
        partial_value = (pass_grad(partial_value).astype(jnp.float32) + contribution).astype(
            jnp.bfloat16
        )
        return (weight, partial_value, carried)

    weight, partial_value, carried = lax.fori_loop(
        2, cycle_size, one_stop, (weight, partial_value, carried)
    )
    finished = finish_partial(pass_grad(partial_value), own_term)
    out_total, grad_buffer = carried
    summed = lax.psum(finished.astype(jnp.bfloat16), "dp").astype(jnp.float32)
    token_count = row_count * cycle_size * lax.axis_size("dp")
    return (out_total.astype(jnp.bfloat16), grad_buffer, summed / math.sqrt(token_count))


def solution(mesh):
    in_specs = (P(("dp", "blk"), None), P(("dp", "blk"), None), P("blk", None))
    out_specs = (P(("dp", "blk"), None), P(("dp", "blk"), None), P("blk", None))
    return jax.shard_map(body, mesh=mesh, in_specs=in_specs, out_specs=out_specs, check_vma=False)
```

profile of v0, /device:TPU:1, one launch (start us, length us, event | category | flops | bytes accessed | tf_op | source)
XLA Modules:
  0.0 725.1 jit_solution(6232754334397640442)
XLA Ops:
  7.2 4.4 collective-permute-start.2
  11.6 4.5 fusion.14
  20.4 5.9 collective-permute-done.2
  28.4 498.7 %while.21 = (s32[]{:T(128)}, bf16[128,1024]{1,0:T(8,128)(2,1)S(1)}, bf16[128,1024]{1,0:T(8,128)(2,1)}, f32[192,1024]{1,0:T(8,128)S(1)}, bf16[192,4096]{1,0:T(8,1...) while((s32[]{:T(128)}, bf16[128,1024]{1,0:T(8,128)(2,1)S(1)}, ...), condition=%wide.region_1.2_spmd, body=%wide.region_0.1_spmd.sunk | while | flops 151633936 | bytes 6275492 | solution.py:85
  32.3 6.7 collective-permute-done
  39.3 5.3 collective-permute-done.1
  51.2 5.8 collective-permute-done
  57.3 5.3 collective-permute-done.1
  69.2 5.3 collective-permute-done
  74.9 4.8 collective-permute-done.1
  86.3 5.3 collective-permute-done
  102.4 5.3 collective-permute-done
  117.7 5.3 collective-permute-done
  132.5 5.3 collective-permute-done
  148.3 4.2 collective-permute-done
  160.9 4.0 collective-permute-start.1
  177.0 4.4 collective-permute-start.1
  189.1 5.1 collective-permute-start
  199.3 4.4 collective-permute-done.1
  206.4 4.5 collective-permute-start
  211.0 4.0 collective-permute-start.1
  215.9 4.5 collective-permute-done.1
  226.1 4.0 collective-permute-start.1
  244.2 4.8 collective-permute-done
  258.5 8.2 %collective-permute-done = bf16[128,1024]{1,0:T(8,128)(2,1)S(1)} collective-permute-done((bf16[128,1024]{1,0:T(8,128)(2,1)S(1)}, bf16[128,1024]{1,0:T(8,128)(2,1)S(1)}, u32[]{:S(2)}, u32[]{:S(2)}) %collective-permute-start) | collective-permute-done | bytes 262176 | tf_op jit(solution)/shard_map/while/body/eval_jaxpr/ppermute | solution.py:14
  267.0 5.3 collective-permute-done.1
  278.9 7.3 %collective-permute-done = bf16[128,1024]{1,0:T(8,128)(2,1)S(1)} collective-permute-done((bf16[128,1024]{1,0:T(8,128)(2,1)S(1)}, bf16[128,1024]{1,0:T(8,128)(2,1)S(1)}, u32[]{:S(2)}, u32[]{:S(2)}) %collective-permute-start) | collective-permute-done | bytes 262176 | tf_op jit(solution)/shard_map/while/body/eval_jaxpr/ppermute | solution.py:14
  286.5 5.3 collective-permute-done.1
  298.5 6.4 collective-permute-done
  305.2 5.3 collective-permute-done.1
  317.1 5.3 collective-permute-done
  322.7 5.5 collective-permute-done.1
  334.8 5.3 collective-permute-done
  340.5 4.5 collective-permute-done.1
  351.6 5.3 collective-permute-done
  367.5 5.3 collective-permute-done
  382.3 5.5 collective-permute-done
  397.2 5.3 collective-permute-done
  412.0 5.3 collective-permute-done
  426.7 5.3 collective-permute-done
  441.5 6.3 collective-permute-done
  457.5 7.1 collective-permute-done
  474.0 8.5 %collective-permute-done = bf16[128,1024]{1,0:T(8,128)(2,1)S(1)} collective-permute-done((bf16[128,1024]{1,0:T(8,128)(2,1)S(1)}, bf16[128,1024]{1,0:T(8,128)(2,1)S(1)}, u32[]{:S(2)}, u32[]{:S(2)}) %collective-permute-start) | collective-permute-done | bytes 262176 | tf_op jit(solution)/shard_map/while/body/eval_jaxpr/ppermute | solution.py:14
  491.9 8.5 %collective-permute-done = bf16[128,1024]{1,0:T(8,128)(2,1)S(1)} collective-permute-done((bf16[128,1024]{1,0:T(8,128)(2,1)S(1)}, bf16[128,1024]{1,0:T(8,128)(2,1)S(1)}, u32[]{:S(2)}, u32[]{:S(2)}) %collective-permute-start) | collective-permute-done | bytes 262176 | tf_op jit(solution)/shard_map/while/body/eval_jaxpr/ppermute | solution.py:14
  510.9 8.3 %collective-permute-done = bf16[128,1024]{1,0:T(8,128)(2,1)S(1)} collective-permute-done((bf16[128,1024]{1,0:T(8,128)(2,1)S(1)}, bf16[128,1024]{1,0:T(8,128)(2,1)S(1)}, u32[]{:S(2)}, u32[]{:S(2)}) %collective-permute-start) | collective-permute-done | bytes 262176 | tf_op jit(solution)/shard_map/while/body/eval_jaxpr/ppermute | solution.py:14
  519.5 4.8 collective-permute-done.1
  529.2 9.8 %collective-permute-done.3 = bf16[128,1024]{1,0:T(8,128)(2,1)S(1)} collective-permute-done((bf16[128,1024]{1,0:T(8,128)(2,1)}, bf16[128,1024]{1,0:T(8,128)(2,1)S(1)}, u32[]{:S(2)}, u32[]{:S(2)}) %collective-permute-start.3) | collective-permute-done | bytes 262176 | tf_op jit(solution)/shard_map/ppermute | solution.py:14
  540.6 175.8 %all-reduce.2.cloned.1.call-done = bf16[128,1024]{1,0:T(8,128)(2,1)} async-done(((bf16[128,1024]{1,0:T(8,128)(2,1)}), bf16[128,1024]{1,0:T(8,128)(2,1)}) %all-reduce.2.cloned.1.call-update) | async-done | bytes 262160 | tf_op jit(solution)/shard_map/psum | solution.py:90
  (215 shorter events, 276.1 us)
Async XLA Ops:
  7.2 709.2 %all-reduce.2.cloned.1.call-start = ((), (), s32[]{:S(2)}) async-start(), calls=%async_computation | async-start | bytes 524288 | tf_op jit(solution)/shard_map/psum | solution.py:90
  7.2 19.1 %collective-permute-start.2 = (bf16[128,1024]{1,0:T(8,128)(2,1)}, bf16[128,1024]{1,0:T(8,128)(2,1)S(1)}, u32[]{:S(2)}, u32[]{:S(2)}) collective-permute-start(bf16[128,1024]{1,0:T(8,128)(2,1)} %param.7), channel_id=1, source_target_pairs={{0,1},{1,2},{2,3},{3,4},{4,5},{5,6},{6,7},{7,8},{8,9},{9,10},{10,1... | collective-permute-start | bytes 786440 | tf_op jit(solution)/shard_map/ppermute | solution.py:14
  28.4 10.6 %collective-permute-start = (bf16[128,1024]{1,0:T(8,128)(2,1)S(1)}, bf16[128,1024]{1,0:T(8,128)(2,1)S(1)}, u32[]{:S(2)}, u32[]{:S(2)}) collective-permute-start(bf16[128,1024]{1,0:T(8,128)(2,1)S(1)} %get-tuple-element.321), channel_id=1, source_target_pairs={{0,1},{1,2},{2,3},{3,4},{4,5},{5,6},{6,7},{7,8},{8,9},{9,10},{10,1... | collective-permute-start | bytes 786440 | tf_op jit(solution)/shard_map/while/body/eval_jaxpr/ppermute | solution.py:14
  30.3 14.3 %collective-permute-start.1 = (bf16[128,1024]{1,0:T(8,128)(2,1)}, bf16[128,1024]{1,0:T(8,128)(2,1)S(1)}, u32[]{:S(2)}, u32[]{:S(2)}) collective-permute-start(bf16[128,1024]{1,0:T(8,128)(2,1)} %get-tuple-element.322), channel_id=1, source_target_pairs={{0,1},{1,2},{2,3},{3,4},{4,5},{5,6},{6,7},{7,8},{8,9},{9,10},{10,1... | collective-permute-start | bytes 786440 | tf_op jit(solution)/shard_map/while/body/eval_jaxpr/ppermute | solution.py:14
  47.3 9.6 %collective-permute-start = (bf16[128,1024]{1,0:T(8,128)(2,1)S(1)}, bf16[128,1024]{1,0:T(8,128)(2,1)S(1)}, u32[]{:S(2)}, u32[]{:S(2)}) collective-permute-start(bf16[128,1024]{1,0:T(8,128)(2,1)S(1)} %get-tuple-element.321), channel_id=1, source_target_pairs={{0,1},{1,2},{2,3},{3,4},{4,5},{5,6},{6,7},{7,8},{8,9},{9,10},{10,1... | collective-permute-start | bytes 786440 | tf_op jit(solution)/shard_map/while/body/eval_jaxpr/ppermute | solution.py:14
  49.3 13.3 %collective-permute-start.1 = (bf16[128,1024]{1,0:T(8,128)(2,1)}, bf16[128,1024]{1,0:T(8,128)(2,1)S(1)}, u32[]{:S(2)}, u32[]{:S(2)}) collective-permute-start(bf16[128,1024]{1,0:T(8,128)(2,1)} %get-tuple-element.322), channel_id=1, source_target_pairs={{0,1},{1,2},{2,3},{3,4},{4,5},{5,6},{6,7},{7,8},{8,9},{9,10},{10,1... | collective-permute-start | bytes 786440 | tf_op jit(solution)/shard_map/while/body/eval_jaxpr/ppermute | solution.py:14
  65.3 9.2 %collective-permute-start = (bf16[128,1024]{1,0:T(8,128)(2,1)S(1)}, bf16[128,1024]{1,0:T(8,128)(2,1)S(1)}, u32[]{:S(2)}, u32[]{:S(2)}) collective-permute-start(bf16[128,1024]{1,0:T(8,128)(2,1)S(1)} %get-tuple-element.321), channel_id=1, source_target_pairs={{0,1},{1,2},{2,3},{3,4},{4,5},{5,6},{6,7},{7,8},{8,9},{9,10},{10,1... | collective-permute-start | bytes 786440 | tf_op jit(solution)/shard_map/while/body/eval_jaxpr/ppermute | solution.py:14
  67.3 12.4 %collective-permute-start.1 = (bf16[128,1024]{1,0:T(8,128)(2,1)}, bf16[128,1024]{1,0:T(8,128)(2,1)S(1)}, u32[]{:S(2)}, u32[]{:S(2)}) collective-permute-start(bf16[128,1024]{1,0:T(8,128)(2,1)} %get-tuple-element.322), channel_id=1, source_target_pairs={{0,1},{1,2},{2,3},{3,4},{4,5},{5,6},{6,7},{7,8},{8,9},{9,10},{10,1... | collective-permute-start | bytes 786440 | tf_op jit(solution)/shard_map/while/body/eval_jaxpr/ppermute | solution.py:14
  84.3 11.5 %collective-permute-start.1 = (bf16[128,1024]{1,0:T(8,128)(2,1)}, bf16[128,1024]{1,0:T(8,128)(2,1)S(1)}, u32[]{:S(2)}, u32[]{:S(2)}) collective-permute-start(bf16[128,1024]{1,0:T(8,128)(2,1)} %get-tuple-element.322), channel_id=1, source_target_pairs={{0,1},{1,2},{2,3},{3,4},{4,5},{5,6},{6,7},{7,8},{8,9},{9,10},{10,1... | collective-permute-start | bytes 786440 | tf_op jit(solution)/shard_map/while/body/eval_jaxpr/ppermute | solution.py:14
  100.5 10.6 %collective-permute-start.1 = (bf16[128,1024]{1,0:T(8,128)(2,1)}, bf16[128,1024]{1,0:T(8,128)(2,1)S(1)}, u32[]{:S(2)}, u32[]{:S(2)}) collective-permute-start(bf16[128,1024]{1,0:T(8,128)(2,1)} %get-tuple-element.322), channel_id=1, source_target_pairs={{0,1},{1,2},{2,3},{3,4},{4,5},{5,6},{6,7},{7,8},{8,9},{9,10},{10,1... | collective-permute-start | bytes 786440 | tf_op jit(solution)/shard_map/while/body/eval_jaxpr/ppermute | solution.py:14
  115.7 10.1 %collective-permute-start.1 = (bf16[128,1024]{1,0:T(8,128)(2,1)}, bf16[128,1024]{1,0:T(8,128)(2,1)S(1)}, u32[]{:S(2)}, u32[]{:S(2)}) collective-permute-start(bf16[128,1024]{1,0:T(8,128)(2,1)} %get-tuple-element.322), channel_id=1, source_target_pairs={{0,1},{1,2},{2,3},{3,4},{4,5},{5,6},{6,7},{7,8},{8,9},{9,10},{10,1... | collective-permute-start | bytes 786440 | tf_op jit(solution)/shard_map/while/body/eval_jaxpr/ppermute | solution.py:14
  130.5 10.1 %collective-permute-start.1 = (bf16[128,1024]{1,0:T(8,128)(2,1)}, bf16[128,1024]{1,0:T(8,128)(2,1)S(1)}, u32[]{:S(2)}, u32[]{:S(2)}) collective-permute-start(bf16[128,1024]{1,0:T(8,128)(2,1)} %get-tuple-element.322), channel_id=1, source_target_pairs={{0,1},{1,2},{2,3},{3,4},{4,5},{5,6},{6,7},{7,8},{8,9},{9,10},{10,1... | collective-permute-start | bytes 786440 | tf_op jit(solution)/shard_map/while/body/eval_jaxpr/ppermute | solution.py:14
  145.3 10.1 %collective-permute-start.1 = (bf16[128,1024]{1,0:T(8,128)(2,1)}, bf16[128,1024]{1,0:T(8,128)(2,1)S(1)}, u32[]{:S(2)}, u32[]{:S(2)}) collective-permute-start(bf16[128,1024]{1,0:T(8,128)(2,1)} %get-tuple-element.322), channel_id=1, source_target_pairs={{0,1},{1,2},{2,3},{3,4},{4,5},{5,6},{6,7},{7,8},{8,9},{9,10},{10,1... | collective-permute-start | bytes 786440 | tf_op jit(solution)/shard_map/while/body/eval_jaxpr/ppermute | solution.py:14
  160.9 9.4 %collective-permute-start.1 = (bf16[128,1024]{1,0:T(8,128)(2,1)}, bf16[128,1024]{1,0:T(8,128)(2,1)S(1)}, u32[]{:S(2)}, u32[]{:S(2)}) collective-permute-start(bf16[128,1024]{1,0:T(8,128)(2,1)} %get-tuple-element.322), channel_id=1, source_target_pairs={{0,1},{1,2},{2,3},{3,4},{4,5},{5,6},{6,7},{7,8},{8,9},{9,10},{10,1... | collective-permute-start | bytes 786440 | tf_op jit(solution)/shard_map/while/body/eval_jaxpr/ppermute | solution.py:14
  173.1 9.6 %collective-permute-start = (bf16[128,1024]{1,0:T(8,128)(2,1)S(1)}, bf16[128,1024]{1,0:T(8,128)(2,1)S(1)}, u32[]{:S(2)}, u32[]{:S(2)}) collective-permute-start(bf16[128,1024]{1,0:T(8,128)(2,1)S(1)} %get-tuple-element.321), channel_id=1, source_target_pairs={{0,1},{1,2},{2,3},{3,4},{4,5},{5,6},{6,7},{7,8},{8,9},{9,10},{10,1... | collective-permute-start | bytes 786440 | tf_op jit(solution)/shard_map/while/body/eval_jaxpr/ppermute | solution.py:14
  177.0 9.4 %collective-permute-start.1 = (bf16[128,1024]{1,0:T(8,128)(2,1)}, bf16[128,1024]{1,0:T(8,128)(2,1)S(1)}, u32[]{:S(2)}, u32[]{:S(2)}) collective-permute-start(bf16[128,1024]{1,0:T(8,128)(2,1)} %get-tuple-element.322), channel_id=1, source_target_pairs={{0,1},{1,2},{2,3},{3,4},{4,5},{5,6},{6,7},{7,8},{8,9},{9,10},{10,1... | collective-permute-start | bytes 786440 | tf_op jit(solution)/shard_map/while/body/eval_jaxpr/ppermute | solution.py:14
  189.1 9.9 %collective-permute-start = (bf16[128,1024]{1,0:T(8,128)(2,1)S(1)}, bf16[128,1024]{1,0:T(8,128)(2,1)S(1)}, u32[]{:S(2)}, u32[]{:S(2)}) collective-permute-start(bf16[128,1024]{1,0:T(8,128)(2,1)S(1)} %get-tuple-element.321), channel_id=1, source_target_pairs={{0,1},{1,2},{2,3},{3,4},{4,5},{5,6},{6,7},{7,8},{8,9},{9,10},{10,1... | collective-permute-start | bytes 786440 | tf_op jit(solution)/shard_map/while/body/eval_jaxpr/ppermute | solution.py:14
  194.2 9.4 %collective-permute-start.1 = (bf16[128,1024]{1,0:T(8,128)(2,1)}, bf16[128,1024]{1,0:T(8,128)(2,1)S(1)}, u32[]{:S(2)}, u32[]{:S(2)}) collective-permute-start(bf16[128,1024]{1,0:T(8,128)(2,1)} %get-tuple-element.322), channel_id=1, source_target_pairs={{0,1},{1,2},{2,3},{3,4},{4,5},{5,6},{6,7},{7,8},{8,9},{9,10},{10,1... | collective-permute-start | bytes 786440 | tf_op jit(solution)/shard_map/while/body/eval_jaxpr/ppermute | solution.py:14
  211.0 9.4 %collective-permute-start.1 = (bf16[128,1024]{1,0:T(8,128)(2,1)}, bf16[128,1024]{1,0:T(8,128)(2,1)S(1)}, u32[]{:S(2)}, u32[]{:S(2)}) collective-permute-start(bf16[128,1024]{1,0:T(8,128)(2,1)} %get-tuple-element.322), channel_id=1, source_target_pairs={{0,1},{1,2},{2,3},{3,4},{4,5},{5,6},{6,7},{7,8},{8,9},{9,10},{10,1... | collective-permute-start | bytes 786440 | tf_op jit(solution)/shard_map/while/body/eval_jaxpr/ppermute | solution.py:14
  226.1 9.4 %collective-permute-start.1 = (bf16[128,1024]{1,0:T(8,128)(2,1)}, bf16[128,1024]{1,0:T(8,128)(2,1)S(1)}, u32[]{:S(2)}, u32[]{:S(2)}) collective-permute-start(bf16[128,1024]{1,0:T(8,128)(2,1)} %get-tuple-element.322), channel_id=1, source_target_pairs={{0,1},{1,2},{2,3},{3,4},{4,5},{5,6},{6,7},{7,8},{8,9},{9,10},{10,1... | collective-permute-start | bytes 786440 | tf_op jit(solution)/shard_map/while/body/eval_jaxpr/ppermute | solution.py:14
  238.2 10.8 %collective-permute-start = (bf16[128,1024]{1,0:T(8,128)(2,1)S(1)}, bf16[128,1024]{1,0:T(8,128)(2,1)S(1)}, u32[]{:S(2)}, u32[]{:S(2)}) collective-permute-start(bf16[128,1024]{1,0:T(8,128)(2,1)S(1)} %get-tuple-element.321), channel_id=1, source_target_pairs={{0,1},{1,2},{2,3},{3,4},{4,5},{5,6},{6,7},{7,8},{8,9},{9,10},{10,1... | collective-permute-start | bytes 786440 | tf_op jit(solution)/shard_map/while/body/eval_jaxpr/ppermute | solution.py:14
  240.2 11.6 %collective-permute-start.1 = (bf16[128,1024]{1,0:T(8,128)(2,1)}, bf16[128,1024]{1,0:T(8,128)(2,1)S(1)}, u32[]{:S(2)}, u32[]{:S(2)}) collective-permute-start(bf16[128,1024]{1,0:T(8,128)(2,1)} %get-tuple-element.322), channel_id=1, source_target_pairs={{0,1},{1,2},{2,3},{3,4},{4,5},{5,6},{6,7},{7,8},{8,9},{9,10},{10,1... | collective-permute-start | bytes 786440 | tf_op jit(solution)/shard_map/while/body/eval_jaxpr/ppermute | solution.py:14
  254.6 12.1 %collective-permute-start = (bf16[128,1024]{1,0:T(8,128)(2,1)S(1)}, bf16[128,1024]{1,0:T(8,128)(2,1)S(1)}, u32[]{:S(2)}, u32[]{:S(2)}) collective-permute-start(bf16[128,1024]{1,0:T(8,128)(2,1)S(1)} %get-tuple-element.321), channel_id=1, source_target_pairs={{0,1},{1,2},{2,3},{3,4},{4,5},{5,6},{6,7},{7,8},{8,9},{9,10},{10,1... | collective-permute-start | bytes 786440 | tf_op jit(solution)/shard_map/while/body/eval_jaxpr/ppermute | solution.py:14
  256.5 15.8 %collective-permute-start.1 = (bf16[128,1024]{1,0:T(8,128)(2,1)}, bf16[128,1024]{1,0:T(8,128)(2,1)S(1)}, u32[]{:S(2)}, u32[]{:S(2)}) collective-permute-start(bf16[128,1024]{1,0:T(8,128)(2,1)} %get-tuple-element.322), channel_id=1, source_target_pairs={{0,1},{1,2},{2,3},{3,4},{4,5},{5,6},{6,7},{7,8},{8,9},{9,10},{10,1... | collective-permute-start | bytes 786440 | tf_op jit(solution)/shard_map/while/body/eval_jaxpr/ppermute | solution.py:14
  275.0 11.2 %collective-permute-start = (bf16[128,1024]{1,0:T(8,128)(2,1)S(1)}, bf16[128,1024]{1,0:T(8,128)(2,1)S(1)}, u32[]{:S(2)}, u32[]{:S(2)}) collective-permute-start(bf16[128,1024]{1,0:T(8,128)(2,1)S(1)} %get-tuple-element.321), channel_id=1, source_target_pairs={{0,1},{1,2},{2,3},{3,4},{4,5},{5,6},{6,7},{7,8},{8,9},{9,10},{10,1... | collective-permute-start | bytes 786440 | tf_op jit(solution)/shard_map/while/body/eval_jaxpr/ppermute | solution.py:14
  276.9 14.9 %collective-permute-start.1 = (bf16[128,1024]{1,0:T(8,128)(2,1)}, bf16[128,1024]{1,0:T(8,128)(2,1)S(1)}, u32[]{:S(2)}, u32[]{:S(2)}) collective-permute-start(bf16[128,1024]{1,0:T(8,128)(2,1)} %get-tuple-element.322), channel_id=1, source_target_pairs={{0,1},{1,2},{2,3},{3,4},{4,5},{5,6},{6,7},{7,8},{8,9},{9,10},{10,1... | collective-permute-start | bytes 786440 | tf_op jit(solution)/shard_map/while/body/eval_jaxpr/ppermute | solution.py:14
  294.6 10.3 %collective-permute-start = (bf16[128,1024]{1,0:T(8,128)(2,1)S(1)}, bf16[128,1024]{1,0:T(8,128)(2,1)S(1)}, u32[]{:S(2)}, u32[]{:S(2)}) collective-permute-start(bf16[128,1024]{1,0:T(8,128)(2,1)S(1)} %get-tuple-element.321), channel_id=1, source_target_pairs={{0,1},{1,2},{2,3},{3,4},{4,5},{5,6},{6,7},{7,8},{8,9},{9,10},{10,1... | collective-permute-start | bytes 786440 | tf_op jit(solution)/shard_map/while/body/eval_jaxpr/ppermute | solution.py:14
  296.5 14.0 %collective-permute-start.1 = (bf16[128,1024]{1,0:T(8,128)(2,1)}, bf16[128,1024]{1,0:T(8,128)(2,1)S(1)}, u32[]{:S(2)}, u32[]{:S(2)}) collective-permute-start(bf16[128,1024]{1,0:T(8,128)(2,1)} %get-tuple-element.322), channel_id=1, source_target_pairs={{0,1},{1,2},{2,3},{3,4},{4,5},{5,6},{6,7},{7,8},{8,9},{9,10},{10,1... | collective-permute-start | bytes 786440 | tf_op jit(solution)/shard_map/while/body/eval_jaxpr/ppermute | solution.py:14
  315.1 13.1 %collective-permute-start.1 = (bf16[128,1024]{1,0:T(8,128)(2,1)}, bf16[128,1024]{1,0:T(8,128)(2,1)S(1)}, u32[]{:S(2)}, u32[]{:S(2)}) collective-permute-start(bf16[128,1024]{1,0:T(8,128)(2,1)} %get-tuple-element.322), channel_id=1, source_target_pairs={{0,1},{1,2},{2,3},{3,4},{4,5},{5,6},{6,7},{7,8},{8,9},{9,10},{10,1... | collective-permute-start | bytes 786440 | tf_op jit(solution)/shard_map/while/body/eval_jaxpr/ppermute | solution.py:14
  332.9 12.1 %collective-permute-start.1 = (bf16[128,1024]{1,0:T(8,128)(2,1)}, bf16[128,1024]{1,0:T(8,128)(2,1)S(1)}, u32[]{:S(2)}, u32[]{:S(2)}) collective-permute-start(bf16[128,1024]{1,0:T(8,128)(2,1)} %get-tuple-element.322), channel_id=1, source_target_pairs={{0,1},{1,2},{2,3},{3,4},{4,5},{5,6},{6,7},{7,8},{8,9},{9,10},{10,1... | collective-permute-start | bytes 786440 | tf_op jit(solution)/shard_map/while/body/eval_jaxpr/ppermute | solution.py:14
  349.7 11.2 %collective-permute-start.1 = (bf16[128,1024]{1,0:T(8,128)(2,1)}, bf16[128,1024]{1,0:T(8,128)(2,1)S(1)}, u32[]{:S(2)}, u32[]{:S(2)}) collective-permute-start(bf16[128,1024]{1,0:T(8,128)(2,1)} %get-tuple-element.322), channel_id=1, source_target_pairs={{0,1},{1,2},{2,3},{3,4},{4,5},{5,6},{6,7},{7,8},{8,9},{9,10},{10,1... | collective-permute-start | bytes 786440 | tf_op jit(solution)/shard_map/while/body/eval_jaxpr/ppermute | solution.py:14
  365.5 10.1 %collective-permute-start.1 = (bf16[128,1024]{1,0:T(8,128)(2,1)}, bf16[128,1024]{1,0:T(8,128)(2,1)S(1)}, u32[]{:S(2)}, u32[]{:S(2)}) collective-permute-start(bf16[128,1024]{1,0:T(8,128)(2,1)} %get-tuple-element.322), channel_id=1, source_target_pairs={{0,1},{1,2},{2,3},{3,4},{4,5},{5,6},{6,7},{7,8},{8,9},{9,10},{10,1... | collective-permute-start | bytes 786440 | tf_op jit(solution)/shard_map/while/body/eval_jaxpr/ppermute | solution.py:14
  378.4 9.4 %collective-permute-start = (bf16[128,1024]{1,0:T(8,128)(2,1)S(1)}, bf16[128,1024]{1,0:T(8,128)(2,1)S(1)}, u32[]{:S(2)}, u32[]{:S(2)}) collective-permute-start(bf16[128,1024]{1,0:T(8,128)(2,1)S(1)} %get-tuple-element.321), channel_id=1, source_target_pairs={{0,1},{1,2},{2,3},{3,4},{4,5},{5,6},{6,7},{7,8},{8,9},{9,10},{10,1... | collective-permute-start | bytes 786440 | tf_op jit(solution)/shard_map/while/body/eval_jaxpr/ppermute | solution.py:14
  380.3 10.3 %collective-permute-start.1 = (bf16[128,1024]{1,0:T(8,128)(2,1)}, bf16[128,1024]{1,0:T(8,128)(2,1)S(1)}, u32[]{:S(2)}, u32[]{:S(2)}) collective-permute-start(bf16[128,1024]{1,0:T(8,128)(2,1)} %get-tuple-element.322), channel_id=1, source_target_pairs={{0,1},{1,2},{2,3},{3,4},{4,5},{5,6},{6,7},{7,8},{8,9},{9,10},{10,1... | collective-permute-start | bytes 786440 | tf_op jit(solution)/shard_map/while/body/eval_jaxpr/ppermute | solution.py:14
  395.2 10.1 %collective-permute-start.1 = (bf16[128,1024]{1,0:T(8,128)(2,1)}, bf16[128,1024]{1,0:T(8,128)(2,1)S(1)}, u32[]{:S(2)}, u32[]{:S(2)}) collective-permute-start(bf16[128,1024]{1,0:T(8,128)(2,1)} %get-tuple-element.322), channel_id=1, source_target_pairs={{0,1},{1,2},{2,3},{3,4},{4,5},{5,6},{6,7},{7,8},{8,9},{9,10},{10,1... | collective-permute-start | bytes 786440 | tf_op jit(solution)/shard_map/while/body/eval_jaxpr/ppermute | solution.py:14
  410.0 10.1 %collective-permute-start.1 = (bf16[128,1024]{1,0:T(8,128)(2,1)}, bf16[128,1024]{1,0:T(8,128)(2,1)S(1)}, u32[]{:S(2)}, u32[]{:S(2)}) collective-permute-start(bf16[128,1024]{1,0:T(8,128)(2,1)} %get-tuple-element.322), channel_id=1, source_target_pairs={{0,1},{1,2},{2,3},{3,4},{4,5},{5,6},{6,7},{7,8},{8,9},{9,10},{10,1... | collective-permute-start | bytes 786440 | tf_op jit(solution)/shard_map/while/body/eval_jaxpr/ppermute | solution.py:14
  424.8 10.1 %collective-permute-start.1 = (bf16[128,1024]{1,0:T(8,128)(2,1)}, bf16[128,1024]{1,0:T(8,128)(2,1)S(1)}, u32[]{:S(2)}, u32[]{:S(2)}) collective-permute-start(bf16[128,1024]{1,0:T(8,128)(2,1)} %get-tuple-element.322), channel_id=1, source_target_pairs={{0,1},{1,2},{2,3},{3,4},{4,5},{5,6},{6,7},{7,8},{8,9},{9,10},{10,1... | collective-permute-start | bytes 786440 | tf_op jit(solution)/shard_map/while/body/eval_jaxpr/ppermute | solution.py:14
  437.6 10.2 %collective-permute-start = (bf16[128,1024]{1,0:T(8,128)(2,1)S(1)}, bf16[128,1024]{1,0:T(8,128)(2,1)S(1)}, u32[]{:S(2)}, u32[]{:S(2)}) collective-permute-start(bf16[128,1024]{1,0:T(8,128)(2,1)S(1)} %get-tuple-element.321), channel_id=1, source_target_pairs={{0,1},{1,2},{2,3},{3,4},{4,5},{5,6},{6,7},{7,8},{8,9},{9,10},{10,1... | collective-permute-start | bytes 786440 | tf_op jit(solution)/shard_map/while/body/eval_jaxpr/ppermute | solution.py:14
  439.5 11.1 %collective-permute-start.1 = (bf16[128,1024]{1,0:T(8,128)(2,1)}, bf16[128,1024]{1,0:T(8,128)(2,1)S(1)}, u32[]{:S(2)}, u32[]{:S(2)}) collective-permute-start(bf16[128,1024]{1,0:T(8,128)(2,1)} %get-tuple-element.322), channel_id=1, source_target_pairs={{0,1},{1,2},{2,3},{3,4},{4,5},{5,6},{6,7},{7,8},{8,9},{9,10},{10,1... | collective-permute-start | bytes 786440 | tf_op jit(solution)/shard_map/while/body/eval_jaxpr/ppermute | solution.py:14
  453.4 11.2 %collective-permute-start = (bf16[128,1024]{1,0:T(8,128)(2,1)S(1)}, bf16[128,1024]{1,0:T(8,128)(2,1)S(1)}, u32[]{:S(2)}, u32[]{:S(2)}) collective-permute-start(bf16[128,1024]{1,0:T(8,128)(2,1)S(1)} %get-tuple-element.321), channel_id=1, source_target_pairs={{0,1},{1,2},{2,3},{3,4},{4,5},{5,6},{6,7},{7,8},{8,9},{9,10},{10,1... | collective-permute-start | bytes 786440 | tf_op jit(solution)/shard_map/while/body/eval_jaxpr/ppermute | solution.py:14
  455.3 12.1 %collective-permute-start.1 = (bf16[128,1024]{1,0:T(8,128)(2,1)}, bf16[128,1024]{1,0:T(8,128)(2,1)S(1)}, u32[]{:S(2)}, u32[]{:S(2)}) collective-permute-start(bf16[128,1024]{1,0:T(8,128)(2,1)} %get-tuple-element.322), channel_id=1, source_target_pairs={{0,1},{1,2},{2,3},{3,4},{4,5},{5,6},{6,7},{7,8},{8,9},{9,10},{10,1... | collective-permute-start | bytes 786440 | tf_op jit(solution)/shard_map/while/body/eval_jaxpr/ppermute | solution.py:14
  470.2 12.4 %collective-permute-start = (bf16[128,1024]{1,0:T(8,128)(2,1)S(1)}, bf16[128,1024]{1,0:T(8,128)(2,1)S(1)}, u32[]{:S(2)}, u32[]{:S(2)}) collective-permute-start(bf16[128,1024]{1,0:T(8,128)(2,1)S(1)} %get-tuple-element.321), channel_id=1, source_target_pairs={{0,1},{1,2},{2,3},{3,4},{4,5},{5,6},{6,7},{7,8},{8,9},{9,10},{10,1... | collective-permute-start | bytes 786440 | tf_op jit(solution)/shard_map/while/body/eval_jaxpr/ppermute | solution.py:14
  472.1 13.2 %collective-permute-start.1 = (bf16[128,1024]{1,0:T(8,128)(2,1)}, bf16[128,1024]{1,0:T(8,128)(2,1)S(1)}, u32[]{:S(2)}, u32[]{:S(2)}) collective-permute-start(bf16[128,1024]{1,0:T(8,128)(2,1)} %get-tuple-element.322), channel_id=1, source_target_pairs={{0,1},{1,2},{2,3},{3,4},{4,5},{5,6},{6,7},{7,8},{8,9},{9,10},{10,1... | collective-permute-start | bytes 786440 | tf_op jit(solution)/shard_map/while/body/eval_jaxpr/ppermute | solution.py:14
  488.0 12.4 %collective-permute-start = (bf16[128,1024]{1,0:T(8,128)(2,1)S(1)}, bf16[128,1024]{1,0:T(8,128)(2,1)S(1)}, u32[]{:S(2)}, u32[]{:S(2)}) collective-permute-start(bf16[128,1024]{1,0:T(8,128)(2,1)S(1)} %get-tuple-element.321), channel_id=1, source_target_pairs={{0,1},{1,2},{2,3},{3,4},{4,5},{5,6},{6,7},{7,8},{8,9},{9,10},{10,1... | collective-permute-start | bytes 786440 | tf_op jit(solution)/shard_map/while/body/eval_jaxpr/ppermute | solution.py:14
  489.9 14.3 %collective-permute-start.1 = (bf16[128,1024]{1,0:T(8,128)(2,1)}, bf16[128,1024]{1,0:T(8,128)(2,1)S(1)}, u32[]{:S(2)}, u32[]{:S(2)}) collective-permute-start(bf16[128,1024]{1,0:T(8,128)(2,1)} %get-tuple-element.322), channel_id=1, source_target_pairs={{0,1},{1,2},{2,3},{3,4},{4,5},{5,6},{6,7},{7,8},{8,9},{9,10},{10,1... | collective-permute-start | bytes 786440 | tf_op jit(solution)/shard_map/while/body/eval_jaxpr/ppermute | solution.py:14
  507.0 12.2 %collective-permute-start = (bf16[128,1024]{1,0:T(8,128)(2,1)S(1)}, bf16[128,1024]{1,0:T(8,128)(2,1)S(1)}, u32[]{:S(2)}, u32[]{:S(2)}) collective-permute-start(bf16[128,1024]{1,0:T(8,128)(2,1)S(1)} %get-tuple-element.321), channel_id=1, source_target_pairs={{0,1},{1,2},{2,3},{3,4},{4,5},{5,6},{6,7},{7,8},{8,9},{9,10},{10,1... | collective-permute-start | bytes 786440 | tf_op jit(solution)/shard_map/while/body/eval_jaxpr/ppermute | solution.py:14
  508.9 15.4 %collective-permute-start.1 = (bf16[128,1024]{1,0:T(8,128)(2,1)}, bf16[128,1024]{1,0:T(8,128)(2,1)S(1)}, u32[]{:S(2)}, u32[]{:S(2)}) collective-permute-start(bf16[128,1024]{1,0:T(8,128)(2,1)} %get-tuple-element.322), channel_id=1, source_target_pairs={{0,1},{1,2},{2,3},{3,4},{4,5},{5,6},{6,7},{7,8},{8,9},{9,10},{10,1... | collective-permute-start | bytes 786440 | tf_op jit(solution)/shard_map/while/body/eval_jaxpr/ppermute | solution.py:14
  527.1 11.9 %collective-permute-start.3 = (bf16[128,1024]{1,0:T(8,128)(2,1)}, bf16[128,1024]{1,0:T(8,128)(2,1)S(1)}, u32[]{:S(2)}, u32[]{:S(2)}) collective-permute-start(bf16[128,1024]{1,0:T(8,128)(2,1)} %get-tuple-element.228), channel_id=1, source_target_pairs={{0,1},{1,2},{2,3},{3,4},{4,5},{5,6},{6,7},{7,8},{8,9},{9,10},{10,1... | collective-permute-start | bytes 786440 | tf_op jit(solution)/shard_map/ppermute | solution.py:14
  (17 other events, 149.8 us)
Sparse Core Ops, SparseCore 0:
  539.9 176.4 all-reduce.1
where the time goes:
time: 728 us; the launch traced here: 725 us
  waiting for transfers between devices  459 us (63%)
  starting transfers between devices  145 us (20%)
  matrix products  95.9 us (13%)
  between operations  14.1 us (2%)
  other arithmetic  7.82 us (1%)
    ppermute x62, waiting for transfers between devices, passed_along(): lax.ppermute(array, axis, [(i, (i + by) % peers) for i in range(peers)])  283 us
    psum x1, waiting for transfers between devices, body(): summed = lax.psum(finished.astype(jnp.bfloat16), 'dp').astype(jnp.float32)  176 us
    ppermute x62, starting transfers between devices, passed_along(): lax.ppermute(array, axis, [(i, (i + by) % peers) for i in range(peers)])  145 us
    dot_general x32, matrix products, visit(): lax.dot_general(out_grad, weight, (((1,), (1,)), ((), ())), preferred_ele...  57.1 us
    dot_general x32, matrix products, visit(): lax.dot_general(hidden_part, out_grad, (((0,), (0,)), ((), ())), preferre...  30.2 us
  transfers between devices with their start and end apart: 63, of which 63 were waited for; matrix products, arithmetic and copies ran while one was open for 3% of the time, Pallas kernels for 0%

commit v1 on v0

v1 whole, which is shorter than its diff:
```python
import math

import jax
import jax.numpy as jnp
from jax import lax
from jax.experimental import pallas as pl
from jax.experimental.pallas import tpu as pltpu
from jax.sharding import PartitionSpec as P

MESH = pl.DeviceIdType.MESH
SQRT_TWO_PI = 0.7978845608028654
CUBIC = 0.044715
F32, BF16 = jnp.float32, jnp.bfloat16
R = 192
D = 1024
BLK = 128
HALF = 64
SHARE = 2048


def gelu_parts(inputs):
    squared = inputs * inputs
    argument = inputs * (SQRT_TWO_PI + (SQRT_TWO_PI * CUBIC) * squared)
    tangent = jnp.tanh(argument)
    gate = 0.5 + 0.5 * tangent
    activation = inputs * gate
    bend = inputs * (0.5 * SQRT_TWO_PI + (1.5 * CUBIC * SQRT_TWO_PI) * squared)
    derivative = gate + (1.0 - tangent * tangent) * bend
    return activation, derivative


def kernel(
    pre_ref, og_ref, w_ref, bo_ref, pg_ref, wgrad_ref,
    xs, hs, ss, gs, wg, ts, ry, rx, rz, acc, bor, pgs, fr, fo,
    in_sem, agd_r, agy_r, agz_s, agx_s, agy_s, rsy_s, rsd_s, rsy_r, rsx_r, rsz_r,
    pgl_sem, pgs_sem, pgr_sem, bo_sem, f1_s, f1_r, f2_s, f2_r,
):
    dp = lax.axis_index("dp")
    blk = lax.axis_index("blk")
    y, xh, c = dp // 4, (dp // 2) % 2, dp % 2
    xl, z = blk // 16, blk % 16
    x = xh * 2 + xl
    yp = y % 2
    q = y * 2 + xh
    is_src = c == xl
    is_sink = c != xl

    def dev(x, y, z, c):
        x, y, z = (x + 4) % 4, (y + 4) % 4, (z + 16) % 16
        return (y * 4 + (x // 2) * 2 + c, (x % 2) * 16 + z)

    sibling = dev(x, y, z, 1 - c)

    def remote(src, dst, send, recv, device):
        return pltpu.make_async_remote_copy(
            src_ref=src, dst_ref=dst, send_sem=send, recv_sem=recv, device_id=device, device_id_type=MESH
        )

    z_cols = pl.ds(pl.multiple_of(yp * 256, 128), 768)
    x_cols = pl.ds(pl.multiple_of(yp * 384, 128), 640)
    src_own, src_other = (pl.ds(pl.multiple_of(k * 768, 128), 256) for k in (yp, 1 - yp))
    sink_own, sink_other = (pl.ds(pl.multiple_of(k * 640, 128), 384) for k in (yp, 1 - yp))

    mine = pl.ds(pl.multiple_of(c * SHARE, SHARE), SHARE)
    theirs = pl.ds(pl.multiple_of((1 - c) * SHARE, SHARE), SHARE)
    load_x = pltpu.make_async_copy(pre_ref.at[:, mine], xs.at[pl.ds(0, R)], in_sem.at[0])
    load_g = pltpu.make_async_copy(og_ref, gs.at[pl.ds(0, R)], in_sem.at[1])
    load_w = pltpu.make_async_copy(w_ref.at[:, z_cols], wg.at[0, pl.ds(0, BLK), z_cols], in_sem.at[2])

    @pl.when(is_src)
    def _():
        load_w.start()

    load_x.start()
    load_g.start()

    barrier = pltpu.get_barrier_semaphore()
    peers = [dev(x, y, z + 1, c), dev(x, y, z - 1, c), dev(x + 1, y, z, c), dev(x - 1, y, z, c), sibling]
    for dy in range(4):
        for dx in (0, 2):
            if dy or dx:
                peers += [dev(x + dx, y + dy, z, c), dev(x + dx, y + dy, z, 1 - c)]
    for peer in peers:
        pl.semaphore_signal(barrier, inc=1, device_id=peer, device_id_type=MESH)
    pl.semaphore_wait(barrier, len(peers))

    swap_x = remote(pre_ref.at[:, theirs], xs.at[pl.ds(R, R)], in_sem.at[3], in_sem.at[4], sibling)
    swap_g = remote(og_ref, gs.at[pl.ds(R, R)], in_sem.at[5], in_sem.at[6], sibling)

    def rows(side, half):
        return pl.ds(side * BLK + half * HALF, HALF)

    def unit(p, side, half):
        return 4 * p + 2 * side + half

    def z_to(side):
        return dev(x, y, z + 1 - 2 * side, c)

    def ag_z(p, side, half, to_p, to_side, way):
        u = unit(to_p, to_side, half)
        return remote(
            wg.at[p, rows(side, half), z_cols], wg.at[to_p, rows(to_side, half), z_cols],
            agz_s.at[u], agd_r.at[u], z_to(way),
        )

    def ag_x(p, side, half):
        u, at = unit(p, side, half), wg.at[p, rows(side, half), x_cols]
        return remote(at, at, agx_s.at[u], agd_r.at[u], dev(x + 1 - 2 * half, y, z, c))

    def ag_y(p, side, half, cols):
        u, at = unit(p, side, half), wg.at[p, rows(side, half), cols]
        return remote(at, at, agy_s.at[u], agy_r.at[u], dev(x, y + 1 - 2 * half, z, c))

    def ag_src(d, half):
        for side in (0, 1):
            ag_z(d, side, half, d, side, side).wait_recv()

            @pl.when(d < 7)
            def _():
                ag_z(d, side, half, d + 1, side, side).start()

            @pl.when((d == 7) & (half == side))
            def _():
                ag_z(d, side, half, 0, 1, side).start()

            ag_x(d, side, half).start()
            ag_y(d, side, half, src_own).start()

    def ag_src_last(half):
        ag_z(0, 1, half, 0, 1, half).wait_recv()
        ag_x(0, 1, half).start()
        ag_y(0, 1, half, src_own).start()

    def ag_sink(p, half, sides=(0, 1)):
        for side in sides:
            ag_x(p, side, half).wait_recv()
            ag_y(p, side, half, sink_own).start()

    def ag_step(m):
        d, half = 1 + m // 2, m % 2
        pl.when(is_src)(lambda: ag_src(d, half))
        pl.when(is_sink)(lambda: ag_sink(d, half))

    def rs_y(p, side, half, cols):
        u = unit(p, side, half)
        return remote(
            ts.at[p, rows(side, half), cols], ry.at[p, rows(side, half), cols],
            rsy_s.at[u], rsy_r.at[u], dev(x, y - 1 + 2 * half, z, c),
        )

    def rs_x(p, side, half):
        u = unit(p, side, half)
        return remote(
            ts.at[p, rows(side, half), x_cols], rx.at[p, rows(side, half), x_cols],
            rsd_s.at[u], rsx_r.at[u], dev(x - 1 + 2 * half, y, z, c),
        )

    def rs_z(p, side, half, to_p, to_side, way):
        u = unit(p, side, half)
        return remote(
            ts.at[p, rows(side, half), z_cols], rz.at[to_p, rows(to_side, half), z_cols],
            rsd_s.at[u], rsz_r.at[unit(to_p, to_side, half)], z_to(1 - way),
        )

    def add(p, at, cols, buffer, from_at=None):
        from_at = at if from_at is None else from_at
        ts[p, at, cols] = ts[p, at, cols] + buffer[p, from_at, cols]

    def rs_y_send(p):
        for side in (0, 1):
            for half in (0, 1):
                pl.when(is_src)(lambda: rs_y(p, side, half, src_other).start())
                pl.when(is_sink)(lambda: rs_y(p, side, half, sink_other).start())

    def rs_sink(p, side, half):
        rs_y(p, side, half, sink_own).wait_recv()
        add(p, rows(side, half), sink_own, ry)
        rs_x(p, side, half).start()

    def rs_local(p, side, half):
        rs_y(p, side, half, src_own).wait_recv()
        add(p, rows(side, half), src_own, ry)
        rs_x(p, side, half).wait_recv()
        add(p, rows(side, half), x_cols, rx)

    def rs_src(p, side, half):
        rs_local(p, side, half)

        @pl.when((p < 7) | (half != side))
        def _():
            rs_z(p, side, half, p, side, side).wait_recv()
            add(p, rows(side, half), z_cols, rz)

        rs_z(p, side, half, p - 1, side, side).start()

    def rs_src_first(half):
        rs_local(0, 1, half)
        rs_z(0, 1, half, 7, 1 - half, 1 - half).start()

    def block_columns(p, side):
        far = jnp.where(p == 0, 8, p)
        zb = (z + far) % 16 if side else (z - p + 16) % 16
        return pl.multiple_of(zb * BLK, BLK)

    def hidden_and_term(p):
        for side in (0, 1):
            cols = pl.ds(block_columns(p, side), BLK)

            @pl.loop(0, 2 * R // 64)
            def _(i):
                at = pl.ds(pl.multiple_of(i * 64, 64), 64)
                activation, derivative = gelu_parts(xs[at, cols].astype(F32))
                hs[p, at, pl.ds(side * BLK, BLK)] = activation.astype(BF16)
                ss[p, at, pl.ds(side * BLK, BLK)] = derivative

        turned = hs[p].T
        for n in range(4):
            cols = pl.ds(n * 256, 256)
            ts[p, :, cols] = jnp.dot(turned, gs[:, cols], preferred_element_type=F32).astype(BF16)

    def pg_copy(p, side, own):
        cols = pl.ds(pl.multiple_of(c * SHARE, SHARE) + block_columns(p, side), BLK)
        part = pgs.at[p, pl.ds(0 if own else R, R), pl.ds(side * BLK, BLK)]
        k = 2 * p + side
        if own:
            return pltpu.make_async_copy(part, pg_ref.at[:, cols], pgl_sem.at[k])
        return remote(part, pg_ref.at[:, cols], pgs_sem.at[k], pgr_sem.at[k], sibling)

    def use_weight(p, first):
        for side in (0, 1):
            for half in (0, 1):
                pl.when(is_src)(lambda: ag_y(p, side, half, src_other).wait_recv())
                pl.when(is_sink)(lambda: ag_y(p, side, half, sink_other).wait_recv())
        weight = wg.at[p]
        d_hidden = lax.dot_general(gs[...], weight[...], (((1,), (1,)), ((), ())), preferred_element_type=F32)
        pgs[p] = (d_hidden * ss[p]).astype(BF16)
        for side in (0, 1):
            pg_copy(p, side, False).start()
            pg_copy(p, side, True).start()
        for n in range(4):
            cols = pl.ds(n * 256, 256)
            product = jnp.dot(hs[p], weight[:, cols], preferred_element_type=F32)
            acc[:, cols] = product if first else acc[:, cols] + product

    swap_x.start()
    swap_g.start()

    @pl.when(is_src)
    def _():
        load_w.wait()
        for half in (0, 1):
            ag_z(0, 0, half, 1, 0, 0).start()
            ag_z(0, 0, half, 1, 1, 1).start()
        for half in (0, 1):
            ag_x(0, 0, half).start()
            ag_y(0, 0, half, src_own).start()

    load_x.wait()
    load_g.wait()
    swap_x.wait_recv()
    swap_g.wait_recv()

    @pl.loop(0, 8)
    def _(s):
        p = (8 - s) % 8
        hidden_and_term(p)
        rs_y_send(p)

        @pl.when((s == 1) & is_sink)
        def _():
            for half in (0, 1):
                ag_sink(0, half, (0,))

        @pl.when(s >= 2)
        def _():
            ag_step(s - 2)

        @pl.when((s >= 2) & is_sink)
        def _():
            before = (10 - s) % 8
            for half in (0, 1):
                for side in (0, 1):
                    rs_sink(before, side, half)

    @pl.loop(0, 8)
    def _(k):
        @pl.when((k < 2) & is_sink)
        def _():
            for half in (0, 1):
                for side in (0, 1):
                    rs_sink(2 - k, side, half)

        @pl.when((k == 0) & is_src)
        def _():
            for half in (0, 1):
                rs_src_first(half)

        ag_step(6 + k)

        @pl.when((k > 0) & is_src)
        def _():
            for half in (0, 1):
                for side in (0, 1):
                    rs_src(8 - k, side, half)

        @pl.when(k == 1)
        def _():
            use_weight(1, True)

        @pl.when(k > 1)
        def _():
            use_weight(k, False)

    def chip(k):
        return (k % 2) * 2 + xl, k // 2

    def f1(k, sender):
        far_x, far_y = chip(k)
        cols = z_cols
        return remote(
            ts.at[0, pl.ds(16 * k, 16), cols], fr.at[sender, :, cols], f1_s.at[k], f1_r.at[sender], dev(far_x, far_y, z, c)
        )

    def f2(k, core):
        far_x, far_y = chip(k)
        at = fo.at[pl.ds(pl.multiple_of(16 * q, 16), 16)]
        return remote(at, at, f2_s.at[2 * k + core], f2_r.at[q], dev(far_x, far_y, z, core))

    def f2_arrival(k):
        at = fo.at[pl.ds(16 * k, 16)]
        return remote(at, at, f2_s.at[2 * k], f2_r.at[k], sibling)

    @pl.when(is_src)
    def _():
        for half in (0, 1):
            ag_src_last(half)
        for half in (0, 1):
            rs_local(0, 0, half)
            for side in (0, 1):
                rs_z(1, side, half, 0, side, side).wait_recv()
                add(0, rows(0, half), z_cols, rz, rows(side, half))
        for k in range(8):

            @pl.when(q != k)
            def _():
                f1(k, q).start()

    @pl.when(is_sink)
    def _():
        for half in (0, 1):
            ag_sink(0, half, (1,))

    @pl.when(is_src)
    def _():
        own_rows = pl.ds(pl.multiple_of(16 * q, 16), 16)
        fr[q, :, z_cols] = ts[0, own_rows, z_cols]
        for k in range(8):

            @pl.when(q != k)
            def _():
                even = k // 2 % 2 == 0
                cols = pl.ds(0 if even else 256, 768)
                remote(fr.at[k, :, cols], fr.at[k, :, cols], f1_s.at[k], f1_r.at[k], sibling).wait_recv()

        def total(keys, cols):
            return sum(fr[k, :, cols].astype(F32) for k in keys)

        even, odd = (0, 1, 4, 5), (2, 3, 6, 7)
        fo[own_rows, pl.ds(0, 256)] = total(even, pl.ds(0, 256)).astype(BF16)
        fo[own_rows, pl.ds(256, 512)] = total(even + odd, pl.ds(256, 512)).astype(BF16)
        fo[own_rows, pl.ds(768, 256)] = total(odd, pl.ds(768, 256)).astype(BF16)
        for k in range(8):
            for core in (0, 1):

                @pl.when((q != k) | (c != core))
                def _():
                    f2(k, core).start()

    use_weight(0, False)
    theirs_out = remote(acc.at[pl.ds(R, R)], bor, bo_sem.at[0], bo_sem.at[1], sibling)
    theirs_out.start()
    for k in range(8):

        @pl.when((q != k) | is_sink)
        def _():
            f2_arrival(k).wait_recv()

    wgrad_ref[...] = fo[...].astype(F32) * (1.0 / math.sqrt(98304))
    theirs_out.wait_recv()
    bo_ref[...] = (acc[pl.ds(0, R)] + bor[...]).astype(BF16)

    swap_x.wait_send()
    swap_g.wait_send()
    theirs_out.wait_send()

    @pl.loop(0, 8)
    def _(p):
        for side in (0, 1):
            pg_copy(p, side, True).wait()
            pg_copy(p, side, False).wait()
            for half in (0, 1):

                @pl.when(is_src)
                def _():
                    ag_x(p, side, half).wait_send()
                    ag_y(p, side, half, src_own).wait_send()
                    rs_y(p, side, half, src_other).wait_send()

                    @pl.when((p > 0) | (side == 1))
                    def _():
                        ag_z(p, side, half, p, side, side).wait_send()
                        rs_z(p, side, half, p, side, side).wait_send()

                @pl.when(is_sink)
                def _():
                    ag_y(p, side, half, sink_own).wait_send()
                    rs_y(p, side, half, sink_other).wait_send()
                    rs_x(p, side, half).wait_send()

    @pl.when(is_src)
    def _():
        for k in range(8):

            @pl.when(q != k)
            def _():
                f1(k, q).wait_send()

            for core in (0, 1):

                @pl.when((q != k) | (c != core))
                def _():
                    f2(k, core).wait_send()


def body(pre_gelu, out_grad, down_weight):
    dma = pltpu.SemaphoreType.DMA
    vmem = pltpu.VMEM
    hbm = pl.BlockSpec(memory_space=pl.ANY)
    return pl.pallas_call(
        kernel,
        out_shape=(
            jax.ShapeDtypeStruct((R, D), BF16),
            jax.ShapeDtypeStruct((R, 2 * SHARE), BF16),
            jax.ShapeDtypeStruct((BLK, D), F32),
        ),
        in_specs=[hbm, hbm, hbm],
        out_specs=(
            pl.BlockSpec(memory_space=vmem),
            hbm,
            pl.BlockSpec(memory_space=vmem),
        ),
        scratch_shapes=[
            vmem((2 * R, SHARE), BF16),
            vmem((8, 2 * R, 256), BF16),
            vmem((8, 2 * R, 256), F32),
            vmem((2 * R, D), BF16),
            vmem((8, 256, D), BF16),
            vmem((8, 256, D), BF16),
            vmem((8, 256, D), BF16),
            vmem((8, 256, D), BF16),
            vmem((8, 256, D), BF16),
            vmem((2 * R, D), F32),
            vmem((R, D), F32),
            vmem((8, 2 * R, 256), BF16),
            vmem((8, 16, D), BF16),
            vmem((BLK, D), BF16),
            dma((7,)),
            *[dma((32,)) for _ in range(10)],
            dma((16,)),
            dma((16,)),
            dma((16,)),
            dma((2,)),
            dma((8,)),
            dma((8,)),
            dma((16,)),
            dma((8,)),
        ],
        compiler_params=pltpu.CompilerParams(
            collective_id=0, has_side_effects=True, vmem_limit_bytes=56 * 1024 * 1024
        ),
        cost_estimate=pl.CostEstimate(flops=4831838208, bytes_accessed=4 << 20, transcendentals=786432),
        name="fused",
    )(pre_gelu, out_grad, down_weight)


def solution(mesh):
    in_specs = (P(("dp", "blk"), None), P(("dp", "blk"), None), P("blk", None))
    out_specs = (P(("dp", "blk"), None), P(("dp", "blk"), None), P("blk", None))
    return jax.shard_map(body, mesh=mesh, in_specs=in_specs, out_specs=out_specs, check_vma=False)
```

time: 728 us -> 86.8 us (0.12)
  waiting for transfers between devices: 459 us -> 0 us
  starting transfers between devices: 145 us -> 0 us
  matrix products: 95.9 us -> 0 us
  Pallas kernels: 0 us -> 80.6 us
  between operations: 14.1 us -> 0.64 us
  other arithmetic: 7.82 us -> 0 us
    ppermute x62 -> x0, waiting for transfers between devices: 283 us -> none  [passed_along(): lax.ppermute(array, axis, [(i, (i + by) % peers) for i in range(peers)])]
    psum x1 -> x0, waiting for transfers between devices: 176 us -> none  [body(): summed = lax.psum(finished.astype(jnp.bfloat16), 'dp').astype(jnp.float32)]
    ppermute x62 -> x0, starting transfers between devices: 145 us -> none  [passed_along(): lax.ppermute(array, axis, [(i, (i + by) % peers) for i in range(peers)])]
    dot_general x96 -> x0, matrix products: 95.9 us -> none  [the longest x32 57.1 us: visit(): lax.dot_general(out_grad, weight, (((1,), (1,)), ((), ())), preferred_ele...]
    pallas_call x0 -> x1, Pallas kernels: none -> 80.6 us  [body(): pl.pallas_call(kernel, out_shape=(jax.ShapeDtypeStruct((R, D), BF16), jax...]
  transfers between devices with their start and end apart: 63 -> 0, of which waited for: 63 -> 0; matrix products, arithmetic and copies ran while one was open for 3% -> 0% of each run, Pallas kernels for 0% -> 0%
where the time goes in v1:
time: 86.8 us; the launch traced here: 86.6 us
  Pallas kernels  80.6 us (93%)
  local copies, waits for them, and re-layouts  5.32 us (6%)
    pallas_call x1, Pallas kernels, body(): pl.pallas_call(kernel, out_shape=(jax.ShapeDtypeStruct((R, D), BF16), jax...  80.6 us
    unnamed x5, local copies, waits for them, and re-layouts  5.32 us

profile of v1, /device:TPU:1, one launch (start us, length us, event | category | flops | bytes accessed | tf_op | source)
XLA Modules:
  0.0 86.6 jit_solution(78891143505764805)
XLA Ops:
  0.6 80.6 %fused.1 = (bf16[192,1024]{1,0:T(8,128)(2,1)}, bf16[192,4096]{1,0:T(8,128)(2,1)}, f32[128,1024]{1,0:T(8,128)}) custom-call(bf16[192,4096]{1,0:T(8,128)(2,1)} %pre_ref.1, bf16[192,1024]{1,0:T(8,128)(2,1)} %og_ref.1, bf16[128,1024]{1,0:T(8,128)(2,1)} %w_ref.1), custom_call_target="tpu_custom_call" | custom-call | flops 4831838208 | bytes 4194304 | tf_op jit(solution)/shard_map/fused/pallas_call | solution.py:439
  81.3 1.8 %copy.9 = bf16[192,1024]{1,0:T(8,128)(2,1)} copy(bf16[192,1024]{1,0:T(8,128)(2,1)} %get-tuple-element.6) | data formatting | bytes 786432
  83.0 0.0 copy-start
  83.0 2.8 %copy.10 = bf16[192,4096]{1,0:T(8,128)(2,1)} copy(bf16[192,4096]{1,0:T(8,128)(2,1)} %get-tuple-element.7) | data formatting | bytes 3145728
  85.8 0.0 copy-done
  85.8 0.8 copy.11
Async XLA Ops:
  83.0 2.8 %copy-start = (f32[128,1024]{1,0:T(8,128)S(1)}, f32[128,1024]{1,0:T(8,128)}, u32[]{:S(2)}) copy-start(f32[128,1024]{1,0:T(8,128)} %get-tuple-element.8) | copy-start | bytes 1572868

commit v2 on v1

--- a/solution.py
+++ b/solution.py
@@ -30,10 +30,10 @@
 
 
 def kernel(
-    pre_ref, og_ref, w_ref, bo_ref, pg_ref, wgrad_ref,
-    xs, hs, ss, gs, wg, ts, ry, rx, rz, acc, bor, pgs, fr, fo,
-    in_sem, agd_r, agy_r, agz_s, agx_s, agy_s, rsy_s, rsd_s, rsy_r, rsx_r, rsz_r,
-    pgl_sem, pgs_sem, pgr_sem, bo_sem, f1_s, f1_r, f2_s, f2_r,
+    pre_ref, og_ref, w_ref, bo_ref, pg_ref, fo,
+    xs, hs, ss, gs, wg, ts, ry, rx, rz, acc, bor, pgs, fr,
+    in_sem, sx_s, sx_r, agd_r, agy_r, agz_s, agx_s, agy_s, rsy_s, rsd_s, rsy_r, rsx_r, rsz_r,
+    pgs_sem, pgr_sem, bo_sem, f1_s, f1_r, f2_s, f2_r,
 ):
     dp = lax.axis_index("dp")
     blk = lax.axis_index("blk")
@@ -62,7 +62,6 @@
     sink_own, sink_other = (pl.ds(pl.multiple_of(k * 640, 128), 384) for k in (yp, 1 - yp))
 
     mine = pl.ds(pl.multiple_of(c * SHARE, SHARE), SHARE)
-    theirs = pl.ds(pl.multiple_of((1 - c) * SHARE, SHARE), SHARE)
     load_x = pltpu.make_async_copy(pre_ref.at[:, mine], xs.at[pl.ds(0, R)], in_sem.at[0])
     load_g = pltpu.make_async_copy(og_ref, gs.at[pl.ds(0, R)], in_sem.at[1])
     load_w = pltpu.make_async_copy(w_ref.at[:, z_cols], wg.at[0, pl.ds(0, BLK), z_cols], in_sem.at[2])
@@ -74,6 +73,7 @@
     load_x.start()
     load_g.start()
 
+    acc[...] = jnp.zeros_like(acc)
     barrier = pltpu.get_barrier_semaphore()
     peers = [dev(x, y, z + 1, c), dev(x, y, z - 1, c), dev(x + 1, y, z, c), dev(x - 1, y, z, c), sibling]
     for dy in range(4):
@@ -84,8 +84,17 @@
         pl.semaphore_signal(barrier, inc=1, device_id=peer, device_id_type=MESH)
     pl.semaphore_wait(barrier, len(peers))
 
-    swap_x = remote(pre_ref.at[:, theirs], xs.at[pl.ds(R, R)], in_sem.at[3], in_sem.at[4], sibling)
-    swap_g = remote(og_ref, gs.at[pl.ds(R, R)], in_sem.at[5], in_sem.at[6], sibling)
+    def block_columns(p, side):
+        far = jnp.where(p == 0, 8, p)
+        zb = (z + far) % 16 if side else (z - p + 16) % 16
+        return pl.multiple_of(zb * BLK, BLK)
+
+    swap_g = remote(og_ref, gs.at[pl.ds(R, R)], in_sem.at[3], in_sem.at[4], sibling)
+
+    def swap_x(p, side):
+        at, k = block_columns(p, side), 2 * p + side
+        theirs = pl.ds(pl.multiple_of((1 - c) * SHARE, SHARE) + at, BLK)
+        return remote(pre_ref.at[:, theirs], xs.at[pl.ds(R, R), pl.ds(at, BLK)], sx_s.at[k], sx_r.at[k], sibling)
 
     def rows(side, half):
         return pl.ds(side * BLK + half * HALF, HALF)
@@ -184,8 +193,6 @@
         add(p, rows(side, half), x_cols, rx)
 
     def rs_src(p, side, half):
-        rs_local(p, side, half)
-
         @pl.when((p < 7) | (half != side))
         def _():
             rs_z(p, side, half, p, side, side).wait_recv()
@@ -197,12 +204,7 @@
         rs_local(0, 1, half)
         rs_z(0, 1, half, 7, 1 - half, 1 - half).start()
 
-    def block_columns(p, side):
-        far = jnp.where(p == 0, 8, p)
-        zb = (z + far) % 16 if side else (z - p + 16) % 16
-        return pl.multiple_of(zb * BLK, BLK)
-
-    def hidden_and_term(p):
+    def hidden(p):
         for side in (0, 1):
             cols = pl.ds(block_columns(p, side), BLK)
 
@@ -213,37 +215,45 @@
                 hs[p, at, pl.ds(side * BLK, BLK)] = activation.astype(BF16)
                 ss[p, at, pl.ds(side * BLK, BLK)] = derivative
 
+    def term(p):
         turned = hs[p].T
         for n in range(4):
             cols = pl.ds(n * 256, 256)
             ts[p, :, cols] = jnp.dot(turned, gs[:, cols], preferred_element_type=F32).astype(BF16)
 
-    def pg_copy(p, side, own):
-        cols = pl.ds(pl.multiple_of(c * SHARE, SHARE) + block_columns(p, side), BLK)
-        part = pgs.at[p, pl.ds(0 if own else R, R), pl.ds(side * BLK, BLK)]
+    def pg_columns(p, side):
+        return pl.ds(pl.multiple_of(c * SHARE, SHARE) + block_columns(p, side), BLK)
+
+    def pg_copy(p, side):
         k = 2 * p + side
-        if own:
-            return pltpu.make_async_copy(part, pg_ref.at[:, cols], pgl_sem.at[k])
-        return remote(part, pg_ref.at[:, cols], pgs_sem.at[k], pgr_sem.at[k], sibling)
-
-    def use_weight(p, first):
+        part = pgs.at[p, :, pl.ds(side * BLK, BLK)]
+        return remote(part, pg_ref.at[:, pg_columns(p, side)], pgs_sem.at[k], pgr_sem.at[k], sibling)
+
+    theirs_out = remote(acc.at[pl.ds(R, R)], bor, bo_sem.at[0], bo_sem.at[1], sibling)
+
+    def use_weight(p, last=False):
         for side in (0, 1):
             for half in (0, 1):
                 pl.when(is_src)(lambda: ag_y(p, side, half, src_other).wait_recv())
                 pl.when(is_sink)(lambda: ag_y(p, side, half, sink_other).wait_recv())
         weight = wg.at[p]
+
+        def add_out(at):
+            for n in range(4):
+                cols = pl.ds(n * 256, 256)
+                acc[at, cols] += jnp.dot(hs[p, at, :], weight[:, cols], preferred_element_type=F32)
+
+        if last:
+            add_out(pl.ds(R, R))
+            theirs_out.start()
         d_hidden = lax.dot_general(gs[...], weight[...], (((1,), (1,)), ((), ())), preferred_element_type=F32)
-        pgs[p] = (d_hidden * ss[p]).astype(BF16)
-        for side in (0, 1):
-            pg_copy(p, side, False).start()
-            pg_copy(p, side, True).start()
-        for n in range(4):
-            cols = pl.ds(n * 256, 256)
-            product = jnp.dot(hs[p], weight[:, cols], preferred_element_type=F32)
-            acc[:, cols] = product if first else acc[:, cols] + product
-
-    swap_x.start()
-    swap_g.start()
+        grads = (d_hidden * ss[p]).astype(BF16)
+        pgs[p] = grads[R:]
+        for side in (0, 1):
+            pg_copy(p, side).start()
+        for side in (0, 1):
+            pg_ref[:, pg_columns(p, side)] = grads[:R, side * BLK : (side + 1) * BLK]
+        add_out(pl.ds(0, R) if last else pl.ds(0, 2 * R))
 
     @pl.when(is_src)
     def _():
@@ -251,29 +261,43 @@
         for half in (0, 1):
             ag_z(0, 0, half, 1, 0, 0).start()
             ag_z(0, 0, half, 1, 1, 1).start()
+
+    swap_x(0, 0).start()
+    swap_x(0, 1).start()
+    swap_g.start()
+
+    @pl.loop(1, 8)
+    def _(s):
+        swap_x(8 - s, 0).start()
+        swap_x(8 - s, 1).start()
+
+    @pl.when(is_src)
+    def _():
         for half in (0, 1):
             ag_x(0, 0, half).start()
             ag_y(0, 0, half, src_own).start()
 
     load_x.wait()
     load_g.wait()
-    swap_x.wait_recv()
-    swap_g.wait_recv()
 
     @pl.loop(0, 8)
     def _(s):
         p = (8 - s) % 8
-        hidden_and_term(p)
+        swap_x(p, 0).wait_recv()
+        swap_x(p, 1).wait_recv()
+        hidden(p)
+
+        @pl.when(s == 0)
+        def _():
+            swap_g.wait_recv()
+
+        term(p)
         rs_y_send(p)
 
         @pl.when((s == 1) & is_sink)
         def _():
             for half in (0, 1):
                 ag_sink(0, half, (0,))
-
-        @pl.when(s >= 2)
-        def _():
-            ag_step(s - 2)
 
         @pl.when((s >= 2) & is_sink)
         def _():
@@ -282,44 +306,65 @@
                 for side in (0, 1):
                     rs_sink(before, side, half)
 
-    @pl.loop(0, 8)
-    def _(k):
-        @pl.when((k < 2) & is_sink)
+        @pl.when(s >= 2)
+        def _():
+            ag_step(s - 2)
+
+        @pl.when((s == 6) & is_src)
+        def _():
+            for half in (0, 1):
+                rs_src_first(half)
+
+    @pl.when(is_src)
+    def _():
+        for side in (0, 1):
+            rs_local(7, side, 0)
+
+    @pl.loop(2, 16)
+    def _(n):
+        @pl.when(is_src)
+        def _():
+            for side in (0, 1):
+                rs_src(8 - n // 2, side, n % 2)
+            later = 7 - (n - 1) // 2
+            rs_local(later, 0, (n + 1) % 2)
+
+            @pl.when(later > 0)
+            def _():
+                rs_local(later, 1, (n + 1) % 2)
+
+        @pl.when((n < 4) & is_sink)
         def _():
             for half in (0, 1):
                 for side in (0, 1):
-                    rs_sink(2 - k, side, half)
-
-        @pl.when((k == 0) & is_src)
-        def _():
-            for half in (0, 1):
-                rs_src_first(half)
-
-        ag_step(6 + k)
-
-        @pl.when((k > 0) & is_src)
-        def _():
-            for half in (0, 1):
-                for side in (0, 1):
-                    rs_src(8 - k, side, half)
-
-        @pl.when(k == 1)
-        def _():
-            use_weight(1, True)
-
-        @pl.when(k > 1)
-        def _():
-            use_weight(k, False)
+                    rs_sink(4 - n, side, half)
+
+        @pl.when((n < 13) & ((n - 2) % 3 < 2))
+        def _():
+            ag_step(n + 4 - (n - 2) // 3)
+
+        @pl.when((n == 14) & is_src)
+        def _():
+            for half in (0, 1):
+                ag_src_last(half)
+
+        @pl.when((n % 2 == 1) & (n < 14))
+        def _():
+            use_weight(n // 2)
 
     def chip(k):
         return (k % 2) * 2 + xl, k // 2
 
     def f1(k, sender):
         far_x, far_y = chip(k)
-        cols = z_cols
         return remote(
-            ts.at[0, pl.ds(16 * k, 16), cols], fr.at[sender, :, cols], f1_s.at[k], f1_r.at[sender], dev(far_x, far_y, z, c)
+            ts.at[0, pl.ds(16 * k, 16), z_cols], fr.at[sender, :, z_cols],
+            f1_s.at[k], f1_r.at[sender], dev(far_x, far_y, z, c),
         )
+
+    def f1_arrival(k):
+        at = fr.at[k, :, pl.ds(0 if k // 2 % 2 == 0 else 256, 768)]
+        return remote(at, at, f1_s.at[k], f1_r.at[k], sibling)
 
     def f2(k, core):
         far_x, far_y = chip(k)
@@ -333,34 +378,30 @@
     @pl.when(is_src)
     def _():
         for half in (0, 1):
-            ag_src_last(half)
-        for half in (0, 1):
-            rs_local(0, 0, half)
+            if half:
+                rs_local(0, 0, half)
             for side in (0, 1):
                 rs_z(1, side, half, 0, side, side).wait_recv()
                 add(0, rows(0, half), z_cols, rz, rows(side, half))
-        for k in range(8):
-
-            @pl.when(q != k)
-            def _():
-                f1(k, q).start()
+            for k in range(4 * half, 4 * half + 4):
+
+                @pl.when(q != k)
+                def _():
+                    f1(k, q).start()
 
     @pl.when(is_sink)
     def _():
         for half in (0, 1):
             ag_sink(0, half, (1,))
+
+    use_weight(7)
 
     @pl.when(is_src)
     def _():
         own_rows = pl.ds(pl.multiple_of(16 * q, 16), 16)
         fr[q, :, z_cols] = ts[0, own_rows, z_cols]
         for k in range(8):
-
-            @pl.when(q != k)
-            def _():
-                even = k // 2 % 2 == 0
-                cols = pl.ds(0 if even else 256, 768)
-                remote(fr.at[k, :, cols], fr.at[k, :, cols], f1_s.at[k], f1_r.at[k], sibling).wait_recv()
+            pl.when(q != k)(lambda: f1_arrival(k).wait_recv())
 
         def total(keys, cols):
             return sum(fr[k, :, cols].astype(F32) for k in keys)
@@ -376,28 +417,15 @@
                 def _():
                     f2(k, core).start()
 
-    use_weight(0, False)
-    theirs_out = remote(acc.at[pl.ds(R, R)], bor, bo_sem.at[0], bo_sem.at[1], sibling)
-    theirs_out.start()
-    for k in range(8):
-
-        @pl.when((q != k) | is_sink)
-        def _():
-            f2_arrival(k).wait_recv()
-
-    wgrad_ref[...] = fo[...].astype(F32) * (1.0 / math.sqrt(98304))
-    theirs_out.wait_recv()
-    bo_ref[...] = (acc[pl.ds(0, R)] + bor[...]).astype(BF16)
-
-    swap_x.wait_send()
+    use_weight(0, True)
+
     swap_g.wait_send()
-    theirs_out.wait_send()
 
     @pl.loop(0, 8)
     def _(p):
         for side in (0, 1):
-            pg_copy(p, side, True).wait()
-            pg_copy(p, side, False).wait()
+            swap_x(p, side).wait_send()
+            pg_copy(p, side).wait()
             for half in (0, 1):
 
                 @pl.when(is_src)
@@ -417,38 +445,54 @@
                     rs_y(p, side, half, sink_other).wait_send()
                     rs_x(p, side, half).wait_send()
 
+    theirs_out.wait()
+    bo_ref[...] = (acc[pl.ds(0, R)] + bor[...]).astype(BF16)
+
     @pl.when(is_src)
     def _():
         for k in range(8):
-
-            @pl.when(q != k)
-            def _():
-                f1(k, q).wait_send()
-
+            pl.when(q != k)(lambda: f1(k, q).wait_send())
             for core in (0, 1):
 
                 @pl.when((q != k) | (c != core))
                 def _():
                     f2(k, core).wait_send()
+
+    for k in range(8):
+
+        @pl.when((q != k) | is_sink)
+        def _():
+            f2_arrival(k).wait_recv()
+
+
+def finish(bo_ref, pg_ref, fo_ref, bo_out, pg_out, wgrad_out, scaled, sem):
+    copies = [
+        pltpu.make_async_copy(pg_ref, pg_out, sem.at[0]),
+        pltpu.make_async_copy(bo_ref, bo_out, sem.at[1]),
+        pltpu.make_async_copy(scaled, wgrad_out, sem.at[2]),
+    ]
+    copies[0].start()
+    copies[1].start()
+    scaled[...] = fo_ref[...].astype(F32) * (1.0 / math.sqrt(98304))
+    copies[2].start()
+    for copy in copies:
+        copy.wait()
 
 
 def body(pre_gelu, out_grad, down_weight):
     dma = pltpu.SemaphoreType.DMA
     vmem = pltpu.VMEM
     hbm = pl.BlockSpec(memory_space=pl.ANY)
-    return pl.pallas_call(
+    whole = pl.BlockSpec(memory_space=vmem)
+    results = pl.pallas_call(
         kernel,
         out_shape=(
             jax.ShapeDtypeStruct((R, D), BF16),
             jax.ShapeDtypeStruct((R, 2 * SHARE), BF16),
-            jax.ShapeDtypeStruct((BLK, D), F32),
+            jax.ShapeDtypeStruct((BLK, D), BF16),
         ),
-        in_specs=[hbm, hbm, hbm],
-        out_specs=(
-            pl.BlockSpec(memory_space=vmem),
-            hbm,
-            pl.BlockSpec(memory_space=vmem),
-        ),
+        in_specs=[pl.BlockSpec(memory_space=pltpu.HBM)] * 3,
+        out_specs=(whole, whole, whole),
         scratch_shapes=[
             vmem((2 * R, SHARE), BF16),
             vmem((8, 2 * R, 256), BF16),
@@ -461,12 +505,12 @@
             vmem((8, 256, D), BF16),
             vmem((2 * R, D), F32),
             vmem((R, D), F32),
-            vmem((8, 2 * R, 256), BF16),
+            vmem((8, R, 256), BF16),
             vmem((8, 16, D), BF16),
-            vmem((BLK, D), BF16),
-            dma((7,)),
+            dma((5,)),
+            dma((16,)),
+            dma((16,)),
             *[dma((32,)) for _ in range(10)],
-            dma((16,)),
             dma((16,)),
             dma((16,)),
             dma((2,)),
@@ -476,11 +520,25 @@
             dma((8,)),
         ],
         compiler_params=pltpu.CompilerParams(
-            collective_id=0, has_side_effects=True, vmem_limit_bytes=56 * 1024 * 1024
+            collective_id=0, has_side_effects=True, vmem_limit_bytes=50 * 1024 * 1024
         ),
         cost_estimate=pl.CostEstimate(flops=4831838208, bytes_accessed=4 << 20, transcendentals=786432),
         name="fused",
     )(pre_gelu, out_grad, down_weight)
+    return pl.pallas_call(
+        finish,
+        out_shape=(
+            jax.ShapeDtypeStruct((R, D), BF16),
+            jax.ShapeDtypeStruct((R, 2 * SHARE), BF16),
+            jax.ShapeDtypeStruct((BLK, D), F32),
+        ),
+        in_specs=[whole, whole, whole],
+        out_specs=(hbm, hbm, hbm),
+        scratch_shapes=[vmem((BLK, D), F32), dma((3,))],
+        compiler_params=pltpu.CompilerParams(vmem_limit_bytes=4 * 1024 * 1024),
+        cost_estimate=pl.CostEstimate(flops=131072, bytes_accessed=3 << 20, transcendentals=0),
+        name="finish",
+    )(*results)
 
 
 def solution(mesh):

time: 86.8 us -> 81.6 us (0.940)
  local copies, waits for them, and re-layouts: 5.32 us -> 1.94 us
  Pallas kernels: 80.6 us -> 78.8 us
    unnamed x5 -> x4, local copies, waits for them, and re-layouts: 5.32 us -> 1.94 us
    pallas_call x1, Pallas kernels: 80.6 us -> 77.4 us  [body(): pl.pallas_call(kernel, out_shape=(jax.ShapeDtypeStruct((R, D), BF16), jax...]
    pallas_call x0 -> x1, Pallas kernels: none -> 1.47 us  [body(): pl.pallas_call(finish, out_shape=(jax.ShapeDtypeStruct((R, D), BF16), jax...]
where the time goes in v2:
time: 81.6 us; the launch traced here: 81.4 us
  Pallas kernels  78.8 us (97%)
  local copies, waits for them, and re-layouts  1.94 us (2%)
    pallas_call x1, Pallas kernels, body(): pl.pallas_call(kernel, out_shape=(jax.ShapeDtypeStruct((R, D), BF16), jax...  77.4 us
    unnamed x4, local copies, waits for them, and re-layouts  1.94 us

profile of v2, /device:TPU:1, one launch (start us, length us, event | category | flops | bytes accessed | tf_op | source)
XLA Modules:
  0.0 81.4 jit_solution(13387673939296112902)
XLA Ops:
  0.6 0.0 copy-start
  0.6 1.0 %copy-done = bf16[192,1024]{1,0:T(8,128)(2,1)S(1)} copy-done((bf16[192,1024]{1,0:T(8,128)(2,1)S(1)}, bf16[192,1024]{1,0:T(8,128)(2,1)}, u32[]{:S(2)}) %copy-start) | copy-done | bytes 393240
  1.6 0.0 copy-start.1
  1.6 0.9 %copy-done.1 = bf16[128,1024]{1,0:T(8,128)(2,1)S(1)} copy-done((bf16[128,1024]{1,0:T(8,128)(2,1)S(1)}, bf16[128,1024]{1,0:T(8,128)(2,1)}, u32[]{:S(2)}) %copy-start.1) | copy-done | bytes 262168
  2.6 77.4 %fused.1 = (bf16[192,1024]{1,0:T(8,128)(2,1)S(1)}, bf16[192,4096]{1,0:T(8,128)(2,1)S(1)}, bf16[128,1024]{1,0:T(8,128)(2,1)S(1)}) custom-call(bf16[192,4096]{1,0:T(8,128)(2,1)} %pre_ref.1, bf16[192,1024]{1,0:T(8,128)(2,1)S(1)} %copy-done, bf16[128,1024]{1,0:T(8,128)(2,1)S(1)} %copy-done.1), custom_call_target="tpu_custom_call" | custom-call | flops 4831838208 | bytes 4194304 | tf_op jit(solution)/shard_map/fused/pallas_call | solution.py:487
  79.9 1.5 %finish.1 = (bf16[192,1024]{1,0:T(8,128)(2,1)}, bf16[192,4096]{1,0:T(8,128)(2,1)}, f32[128,1024]{1,0:T(8,128)}) custom-call(bf16[192,1024]{1,0:T(8,128)(2,1)S(1)} %get-tuple-element.6.bo_ref, bf16[192,4096]{1,0:T(8,128)(2,1)S(1)} %get-tuple-element.7.pg_ref, bf16[128,1024]{1,0:T(8,128)(2,1)S(1)} %get-tuple-element.8.fo_ref), custom_call_target="tpu_custom_call" | custom-call | flops 131072 | bytes 3145728 | tf_op jit(solution)/shard_map/finish/pallas_call | solution.py:528
Async XLA Ops:
  0.6 1.0 %copy-start = (bf16[192,1024]{1,0:T(8,128)(2,1)S(1)}, bf16[192,1024]{1,0:T(8,128)(2,1)}, u32[]{:S(2)}) copy-start(bf16[192,1024]{1,0:T(8,128)(2,1)} %og_ref.1) | copy-start | bytes 1179652
  1.6 0.9 %copy-start.1 = (bf16[128,1024]{1,0:T(8,128)(2,1)S(1)}, bf16[128,1024]{1,0:T(8,128)(2,1)}, u32[]{:S(2)}) copy-start(bf16[128,1024]{1,0:T(8,128)(2,1)} %w_ref.1) | copy-start | bytes 786436

commit v3 on v2

--- a/solution.py
+++ b/solution.py
@@ -15,6 +15,8 @@
 D = 1024
 BLK = 128
 HALF = 64
+AG_PARTS = 1
+RS_PARTS = 2
 SHARE = 2048
 
 
@@ -32,33 +34,41 @@
 def kernel(
     pre_ref, og_ref, w_ref, bo_ref, pg_ref, fo,
     xs, hs, ss, gs, wg, ts, ry, rx, rz, acc, bor, pgs, fr,
-    in_sem, sx_s, sx_r, agd_r, agy_r, agz_s, agx_s, agy_s, rsy_s, rsd_s, rsy_r, rsx_r, rsz_r,
+    in_sem, sx_s, sx_r, agx_r, agy_r, agx_s, agy_s, rsy_s, rsx_s, rsy_r, rsx_r, agz_s, agz_r, rsz_s, rsz_r,
     pgs_sem, pgr_sem, bo_sem, f1_s, f1_r, f2_s, f2_r,
 ):
     dp = lax.axis_index("dp")
     blk = lax.axis_index("blk")
     y, xh, c = dp // 4, (dp // 2) % 2, dp % 2
     xl, z = blk // 16, blk % 16
-    x = xh * 2 + xl
     yp = y % 2
     q = y * 2 + xh
     is_src = c == xl
     is_sink = c != xl
 
-    def dev(x, y, z, c):
-        x, y, z = (x + 4) % 4, (y + 4) % 4, (z + 16) % 16
-        return (y * 4 + (x // 2) * 2 + c, (x % 2) * 16 + z)
-
-    sibling = dev(x, y, z, 1 - c)
+    z_next = [(dp, xl * 16 + (z + 1) % 16), (dp, xl * 16 + (z + 15) % 16)]
+    x_same, x_flip = xh * 2, (1 - xh) * 2
+    x_blk = (1 - xl) * 16 + z
+    x_next = [
+        (y * 4 + jnp.where(xl == 0, x_same, x_flip) + c, x_blk),
+        (y * 4 + jnp.where(xl == 0, x_flip, x_same) + c, x_blk),
+    ]
+    y_next = [((y + 1) % 4 * 4 + dp % 4, blk), ((y + 3) % 4 * 4 + dp % 4, blk)]
+    sibling = (dp + 1 - 2 * c, blk)
+
+    def pick(pair, down):
+        if isinstance(down, int):
+            return pair[down]
+        return tuple(jnp.where(down == 0, a, b) for a, b in zip(*pair))
 
     def remote(src, dst, send, recv, device):
         return pltpu.make_async_remote_copy(
             src_ref=src, dst_ref=dst, send_sem=send, recv_sem=recv, device_id=device, device_id_type=MESH
         )
 
-    z_cols = pl.ds(pl.multiple_of(yp * 256, 128), 768)
+    z_cols = pl.ds(pl.multiple_of(yp * 384, 128), 640)
     x_cols = pl.ds(pl.multiple_of(yp * 384, 128), 640)
-    src_own, src_other = (pl.ds(pl.multiple_of(k * 768, 128), 256) for k in (yp, 1 - yp))
+    src_own, src_other = (pl.ds(pl.multiple_of(k * 640, 128), 384) for k in (yp, 1 - yp))
     sink_own, sink_other = (pl.ds(pl.multiple_of(k * 640, 128), 384) for k in (yp, 1 - yp))
 
     mine = pl.ds(pl.multiple_of(c * SHARE, SHARE), SHARE)
@@ -75,14 +85,15 @@
 
     acc[...] = jnp.zeros_like(acc)
     barrier = pltpu.get_barrier_semaphore()
-    peers = [dev(x, y, z + 1, c), dev(x, y, z - 1, c), dev(x + 1, y, z, c), dev(x - 1, y, z, c), sibling]
-    for dy in range(4):
-        for dx in (0, 2):
-            if dy or dx:
-                peers += [dev(x + dx, y + dy, z, c), dev(x + dx, y + dy, z, 1 - c)]
-    for peer in peers:
+    for peer in z_next + x_next:
         pl.semaphore_signal(barrier, inc=1, device_id=peer, device_id_type=MESH)
-    pl.semaphore_wait(barrier, len(peers))
+    for k in range(16):
+
+        @pl.when(dp != k)
+        def _():
+            pl.semaphore_signal(barrier, inc=1, device_id=(k, blk), device_id_type=MESH)
+
+    pl.semaphore_wait(barrier, 19)
 
     def block_columns(p, side):
         far = jnp.where(p == 0, 8, p)
@@ -99,44 +110,51 @@
     def rows(side, half):
         return pl.ds(side * BLK + half * HALF, HALF)
 
+    def part_rows(side, half, part, parts):
+        return pl.ds(side * BLK + half * HALF + part * (HALF // parts), HALF // parts)
+
     def unit(p, side, half):
         return 4 * p + 2 * side + half
 
     def z_to(side):
-        return dev(x, y, z + 1 - 2 * side, c)
-
-    def ag_z(p, side, half, to_p, to_side, way):
-        u = unit(to_p, to_side, half)
+        return z_next[side]
+
+    def ag_z(p, side, half, to_p, to_side, way, part):
+        u = AG_PARTS * unit(to_p, to_side, half) + part
         return remote(
-            wg.at[p, rows(side, half), z_cols], wg.at[to_p, rows(to_side, half), z_cols],
-            agz_s.at[u], agd_r.at[u], z_to(way),
+            wg.at[p, part_rows(side, half, part, AG_PARTS), z_cols],
+            wg.at[to_p, part_rows(to_side, half, part, AG_PARTS), z_cols],
+            agz_s.at[u], agz_r.at[u], z_to(way),
         )
 
     def ag_x(p, side, half):
         u, at = unit(p, side, half), wg.at[p, rows(side, half), x_cols]
-        return remote(at, at, agx_s.at[u], agd_r.at[u], dev(x + 1 - 2 * half, y, z, c))
+        return remote(at, at, agx_s.at[u], agx_r.at[u], pick(x_next, half))
 
     def ag_y(p, side, half, cols):
         u, at = unit(p, side, half), wg.at[p, rows(side, half), cols]
-        return remote(at, at, agy_s.at[u], agy_r.at[u], dev(x, y + 1 - 2 * half, z, c))
+        return remote(at, at, agy_s.at[u], agy_r.at[u], pick(y_next, half))
 
     def ag_src(d, half):
+        for part in range(AG_PARTS):
+            for side in (0, 1):
+                ag_z(d, side, half, d, side, side, part).wait_recv()
+
+                @pl.when(d < 7)
+                def _():
+                    ag_z(d, side, half, d + 1, side, side, part).start()
+
+                @pl.when((d == 7) & (half == side))
+                def _():
+                    ag_z(d, side, half, 0, 1, side, part).start()
+
         for side in (0, 1):
-            ag_z(d, side, half, d, side, side).wait_recv()
-
-            @pl.when(d < 7)
-            def _():
-                ag_z(d, side, half, d + 1, side, side).start()
-
-            @pl.when((d == 7) & (half == side))
-            def _():
-                ag_z(d, side, half, 0, 1, side).start()
-
             ag_x(d, side, half).start()
             ag_y(d, side, half, src_own).start()
 
     def ag_src_last(half):
-        ag_z(0, 1, half, 0, 1, half).wait_recv()
+        for part in range(AG_PARTS):
+            ag_z(0, 1, half, 0, 1, half, part).wait_recv()
         ag_x(0, 1, half).start()
         ag_y(0, 1, half, src_own).start()
 
@@ -145,30 +163,26 @@
             ag_x(p, side, half).wait_recv()
             ag_y(p, side, half, sink_own).start()
 
-    def ag_step(m):
-        d, half = 1 + m // 2, m % 2
-        pl.when(is_src)(lambda: ag_src(d, half))
-        pl.when(is_sink)(lambda: ag_sink(d, half))
-
     def rs_y(p, side, half, cols):
         u = unit(p, side, half)
         return remote(
             ts.at[p, rows(side, half), cols], ry.at[p, rows(side, half), cols],
-            rsy_s.at[u], rsy_r.at[u], dev(x, y - 1 + 2 * half, z, c),
+            rsy_s.at[u], rsy_r.at[u], pick(y_next, 1 - half),
         )
 
     def rs_x(p, side, half):
         u = unit(p, side, half)
         return remote(
             ts.at[p, rows(side, half), x_cols], rx.at[p, rows(side, half), x_cols],
-            rsd_s.at[u], rsx_r.at[u], dev(x - 1 + 2 * half, y, z, c),
+            rsx_s.at[u], rsx_r.at[u], pick(x_next, 1 - half),
         )
 
-    def rs_z(p, side, half, to_p, to_side, way):
-        u = unit(p, side, half)
+    def rs_z(p, side, half, to_p, to_side, way, part):
         return remote(
-            ts.at[p, rows(side, half), z_cols], rz.at[to_p, rows(to_side, half), z_cols],
-            rsd_s.at[u], rsz_r.at[unit(to_p, to_side, half)], z_to(1 - way),
+            ts.at[p, part_rows(side, half, part, RS_PARTS), z_cols],
+            rz.at[to_p, part_rows(to_side, half, part, RS_PARTS), z_cols],
+            rsz_s.at[RS_PARTS * unit(p, side, half) + part],
+            rsz_r.at[RS_PARTS * unit(to_p, to_side, half) + part], z_to(1 - way),
         )
 
     def add(p, at, cols, buffer, from_at=None):
@@ -176,10 +190,13 @@
         ts[p, at, cols] = ts[p, at, cols] + buffer[p, from_at, cols]
 
     def rs_y_send(p):
-        for side in (0, 1):
-            for half in (0, 1):
-                pl.when(is_src)(lambda: rs_y(p, side, half, src_other).start())
-                pl.when(is_sink)(lambda: rs_y(p, side, half, sink_other).start())
+        def send(cols):
+            for side in (0, 1):
+                for half in (0, 1):
+                    rs_y(p, side, half, cols).start()
+
+        pl.when(is_src)(lambda: send(src_other))
+        pl.when(is_sink)(lambda: send(sink_other))
 
     def rs_sink(p, side, half):
         rs_y(p, side, half, sink_own).wait_recv()
@@ -192,17 +209,21 @@
         rs_x(p, side, half).wait_recv()
         add(p, rows(side, half), x_cols, rx)
 
-    def rs_src(p, side, half):
-        @pl.when((p < 7) | (half != side))
-        def _():
-            rs_z(p, side, half, p, side, side).wait_recv()
-            add(p, rows(side, half), z_cols, rz)
-
-        rs_z(p, side, half, p - 1, side, side).start()
+    def rs_src(p, half):
+        for part in range(RS_PARTS):
+            for side in (0, 1):
+
+                @pl.when((p < 7) | (half != side))
+                def _():
+                    rs_z(p, side, half, p, side, side, part).wait_recv()
+                    add(p, part_rows(side, half, part, RS_PARTS), z_cols, rz)
+
+                rs_z(p, side, half, p - 1, side, side, part).start()
 
     def rs_src_first(half):
         rs_local(0, 1, half)
-        rs_z(0, 1, half, 7, 1 - half, 1 - half).start()
+        for part in range(RS_PARTS):
+            rs_z(0, 1, half, 7, 1 - half, 1 - half, part).start()
 
     def hidden(p):
         for side in (0, 1):
@@ -232,10 +253,13 @@
     theirs_out = remote(acc.at[pl.ds(R, R)], bor, bo_sem.at[0], bo_sem.at[1], sibling)
 
     def use_weight(p, last=False):
-        for side in (0, 1):
-            for half in (0, 1):
-                pl.when(is_src)(lambda: ag_y(p, side, half, src_other).wait_recv())
-                pl.when(is_sink)(lambda: ag_y(p, side, half, sink_other).wait_recv())
+        def arrive(cols):
+            for side in (0, 1):
+                for half in (0, 1):
+                    ag_y(p, side, half, cols).wait_recv()
+
+        pl.when(is_src)(lambda: arrive(src_other))
+        pl.when(is_sink)(lambda: arrive(sink_other))
         weight = wg.at[p]
 
         def add_out(at):
@@ -259,8 +283,9 @@
     def _():
         load_w.wait()
         for half in (0, 1):
-            ag_z(0, 0, half, 1, 0, 0).start()
-            ag_z(0, 0, half, 1, 1, 1).start()
+            for part in range(AG_PARTS):
+                ag_z(0, 0, half, 1, 0, 0, part).start()
+                ag_z(0, 0, half, 1, 1, 1, part).start()
 
     swap_x(0, 0).start()
     swap_x(0, 1).start()
@@ -294,11 +319,6 @@
         term(p)
         rs_y_send(p)
 
-        @pl.when((s == 1) & is_sink)
-        def _():
-            for half in (0, 1):
-                ag_sink(0, half, (0,))
-
         @pl.when((s >= 2) & is_sink)
         def _():
             before = (10 - s) % 8
@@ -306,14 +326,24 @@
                 for side in (0, 1):
                     rs_sink(before, side, half)
 
-        @pl.when(s >= 2)
-        def _():
-            ag_step(s - 2)
-
         @pl.when((s == 6) & is_src)
         def _():
             for half in (0, 1):
                 rs_src_first(half)
+
+        @pl.when((s > 2) & (s % 2 == 1) & is_src)
+        def _():
+            m = (s - 3) // 2
+            ag_src(1 + m // 2, m % 2)
+
+        @pl.when((s == 5) & is_sink)
+        def _():
+            for half in (0, 1):
+                ag_sink(0, half, (0,))
+
+        @pl.when((s == 7) & is_sink)
+        def _():
+            ag_sink(1, 0)
 
     @pl.when(is_src)
     def _():
@@ -324,8 +354,7 @@
     def _(n):
         @pl.when(is_src)
         def _():
-            for side in (0, 1):
-                rs_src(8 - n // 2, side, n % 2)
+            rs_src(8 - n // 2, n % 2)
             later = 7 - (n - 1) // 2
             rs_local(later, 0, (n + 1) % 2)
 
@@ -339,37 +368,36 @@
                 for side in (0, 1):
                     rs_sink(4 - n, side, half)
 
-        @pl.when((n < 13) & ((n - 2) % 3 < 2))
-        def _():
-            ag_step(n + 4 - (n - 2) // 3)
+        @pl.when((n < 13) & is_src)
+        def _():
+            ag_src((n + 3) // 2, (n + 1) % 2)
+
+        @pl.when((n < 15) & is_sink)
+        def _():
+            ag_sink((n + 1) // 2, (n + 1) % 2)
 
         @pl.when((n == 14) & is_src)
         def _():
             for half in (0, 1):
                 ag_src_last(half)
 
-        @pl.when((n % 2 == 1) & (n < 14))
-        def _():
-            use_weight(n // 2)
-
-    def chip(k):
-        return (k % 2) * 2 + xl, k // 2
+        @pl.when((n % 2 == 1) & (n > 4))
+        def _():
+            use_weight((n - 3) // 2)
 
     def f1(k, sender):
-        far_x, far_y = chip(k)
         return remote(
             ts.at[0, pl.ds(16 * k, 16), z_cols], fr.at[sender, :, z_cols],
-            f1_s.at[k], f1_r.at[sender], dev(far_x, far_y, z, c),
+            f1_s.at[k], f1_r.at[sender], (2 * k + c, blk),
         )
 
     def f1_arrival(k):
-        at = fr.at[k, :, pl.ds(0 if k // 2 % 2 == 0 else 256, 768)]
+        at = fr.at[k, :, pl.ds(0 if k // 2 % 2 == 0 else 384, 640)]
         return remote(at, at, f1_s.at[k], f1_r.at[k], sibling)
 
     def f2(k, core):
-        far_x, far_y = chip(k)
         at = fo.at[pl.ds(pl.multiple_of(16 * q, 16), 16)]
-        return remote(at, at, f2_s.at[2 * k + core], f2_r.at[q], dev(far_x, far_y, z, core))
+        return remote(at, at, f2_s.at[2 * k + core], f2_r.at[q], (2 * k + core, blk))
 
     def f2_arrival(k):
         at = fo.at[pl.ds(16 * k, 16)]
@@ -381,7 +409,8 @@
             if half:
                 rs_local(0, 0, half)
             for side in (0, 1):
-                rs_z(1, side, half, 0, side, side).wait_recv()
+                for part in range(RS_PARTS):
+                    rs_z(1, side, half, 0, side, side, part).wait_recv()
                 add(0, rows(0, half), z_cols, rz, rows(side, half))
             for k in range(4 * half, 4 * half + 4):
 
@@ -407,9 +436,9 @@
             return sum(fr[k, :, cols].astype(F32) for k in keys)
 
         even, odd = (0, 1, 4, 5), (2, 3, 6, 7)
-        fo[own_rows, pl.ds(0, 256)] = total(even, pl.ds(0, 256)).astype(BF16)
-        fo[own_rows, pl.ds(256, 512)] = total(even + odd, pl.ds(256, 512)).astype(BF16)
-        fo[own_rows, pl.ds(768, 256)] = total(odd, pl.ds(768, 256)).astype(BF16)
+        fo[own_rows, pl.ds(0, 384)] = total(even, pl.ds(0, 384)).astype(BF16)
+        fo[own_rows, pl.ds(384, 256)] = total(even + odd, pl.ds(384, 256)).astype(BF16)
+        fo[own_rows, pl.ds(640, 384)] = total(odd, pl.ds(640, 384)).astype(BF16)
         for k in range(8):
             for core in (0, 1):
 
@@ -426,21 +455,30 @@
         for side in (0, 1):
             swap_x(p, side).wait_send()
             pg_copy(p, side).wait()
-            for half in (0, 1):
-
-                @pl.when(is_src)
-                def _():
+
+        @pl.when(is_src)
+        def _():
+            for side in (0, 1):
+                for half in (0, 1):
                     ag_x(p, side, half).wait_send()
                     ag_y(p, side, half, src_own).wait_send()
                     rs_y(p, side, half, src_other).wait_send()
 
-                    @pl.when((p > 0) | (side == 1))
-                    def _():
-                        ag_z(p, side, half, p, side, side).wait_send()
-                        rs_z(p, side, half, p, side, side).wait_send()
-
-                @pl.when(is_sink)
-                def _():
+                def sent_z(half):
+                    for part in range(AG_PARTS):
+                        ag_z(p, side, half, p, side, side, part).wait_send()
+                    for part in range(RS_PARTS):
+                        rs_z(p, side, half, p, side, side, part).wait_send()
+
+                @pl.when((p > 0) | (side == 1))
+                def _():
+                    sent_z(0)
+                    sent_z(1)
+
+        @pl.when(is_sink)
+        def _():
+            for side in (0, 1):
+                for half in (0, 1):
                     ag_y(p, side, half, sink_own).wait_send()
                     rs_y(p, side, half, sink_other).wait_send()
                     rs_x(p, side, half).wait_send()
@@ -510,7 +548,9 @@
             dma((5,)),
             dma((16,)),
             dma((16,)),
-            *[dma((32,)) for _ in range(10)],
+            *[dma((32,)) for _ in range(8)],
+            *[dma((32 * AG_PARTS,)) for _ in range(2)],
+            *[dma((32 * RS_PARTS,)) for _ in range(2)],
             dma((16,)),
             dma((16,)),
             dma((2,)),

time: 81.6 us -> 79.8 us (0.978)
  Pallas kernels: 78.8 us -> 77 us
    pallas_call x1, Pallas kernels: 77.4 us -> 75.6 us  [body(): pl.pallas_call(kernel, out_shape=(jax.ShapeDtypeStruct((R, D), BF16), jax...]
where the time goes in v3:
time: 79.8 us; the launch traced here: 79.6 us
  Pallas kernels  77 us (96%)
  local copies, waits for them, and re-layouts  1.94 us (2%)
    pallas_call x1, Pallas kernels, body(): pl.pallas_call(kernel, out_shape=(jax.ShapeDtypeStruct((R, D), BF16), jax...  75.6 us
    unnamed x4, local copies, waits for them, and re-layouts  1.94 us

profile of v3, /device:TPU:1, one launch (start us, length us, event | category | flops | bytes accessed | tf_op | source)
XLA Modules:
  0.0 79.6 jit_solution(11190562095169969574)
XLA Ops:
  0.6 0.0 copy-start
  0.6 1.0 %copy-done = bf16[192,1024]{1,0:T(8,128)(2,1)S(1)} copy-done((bf16[192,1024]{1,0:T(8,128)(2,1)S(1)}, bf16[192,1024]{1,0:T(8,128)(2,1)}, u32[]{:S(2)}) %copy-start) | copy-done | bytes 393240
  1.6 0.0 copy-start.1
  1.6 0.9 %copy-done.1 = bf16[128,1024]{1,0:T(8,128)(2,1)S(1)} copy-done((bf16[128,1024]{1,0:T(8,128)(2,1)S(1)}, bf16[128,1024]{1,0:T(8,128)(2,1)}, u32[]{:S(2)}) %copy-start.1) | copy-done | bytes 262168
  2.6 75.6 %fused.1 = (bf16[192,1024]{1,0:T(8,128)(2,1)S(1)}, bf16[192,4096]{1,0:T(8,128)(2,1)S(1)}, bf16[128,1024]{1,0:T(8,128)(2,1)S(1)}) custom-call(bf16[192,4096]{1,0:T(8,128)(2,1)} %pre_ref.1, bf16[192,1024]{1,0:T(8,128)(2,1)S(1)} %copy-done, bf16[128,1024]{1,0:T(8,128)(2,1)S(1)} %copy-done.1), custom_call_target="tpu_custom_call" | custom-call | flops 4831838208 | bytes 4194304 | tf_op jit(solution)/shard_map/fused/pallas_call | solution.py:525
  78.2 1.5 %finish.1 = (bf16[192,1024]{1,0:T(8,128)(2,1)}, bf16[192,4096]{1,0:T(8,128)(2,1)}, f32[128,1024]{1,0:T(8,128)}) custom-call(bf16[192,1024]{1,0:T(8,128)(2,1)S(1)} %get-tuple-element.6.bo_ref, bf16[192,4096]{1,0:T(8,128)(2,1)S(1)} %get-tuple-element.7.pg_ref, bf16[128,1024]{1,0:T(8,128)(2,1)S(1)} %get-tuple-element.8.fo_ref), custom_call_target="tpu_custom_call" | custom-call | flops 131072 | bytes 3145728 | tf_op jit(solution)/shard_map/finish/pallas_call | solution.py:568
Async XLA Ops:
  0.6 1.0 %copy-start = (bf16[192,1024]{1,0:T(8,128)(2,1)S(1)}, bf16[192,1024]{1,0:T(8,128)(2,1)}, u32[]{:S(2)}) copy-start(bf16[192,1024]{1,0:T(8,128)(2,1)} %og_ref.1) | copy-start | bytes 1179652
  1.6 0.9 %copy-start.1 = (bf16[128,1024]{1,0:T(8,128)(2,1)S(1)}, bf16[128,1024]{1,0:T(8,128)(2,1)}, u32[]{:S(2)}) copy-start(bf16[128,1024]{1,0:T(8,128)(2,1)} %w_ref.1) | copy-start | bytes 786436

commit v4 on v3

--- a/solution.py
+++ b/solution.py
@@ -83,7 +83,6 @@
     load_x.start()
     load_g.start()
 
-    acc[...] = jnp.zeros_like(acc)
     barrier = pltpu.get_barrier_semaphore()
     for peer in z_next + x_next:
         pl.semaphore_signal(barrier, inc=1, device_id=peer, device_id_type=MESH)
@@ -93,6 +92,7 @@
         def _():
             pl.semaphore_signal(barrier, inc=1, device_id=(k, blk), device_id_type=MESH)
 
+    acc[...] = jnp.zeros_like(acc)
     pl.semaphore_wait(barrier, 19)
 
     def block_columns(p, side):
@@ -522,6 +522,7 @@
     vmem = pltpu.VMEM
     hbm = pl.BlockSpec(memory_space=pl.ANY)
     whole = pl.BlockSpec(memory_space=vmem)
+    inputs = [pltpu.with_memory_space_constraint(a, pltpu.HBM) for a in (pre_gelu, out_grad, down_weight)]
     results = pl.pallas_call(
         kernel,
         out_shape=(
@@ -564,7 +565,7 @@
         ),
         cost_estimate=pl.CostEstimate(flops=4831838208, bytes_accessed=4 << 20, transcendentals=786432),
         name="fused",
-    )(pre_gelu, out_grad, down_weight)
+    )(*inputs)
     return pl.pallas_call(
         finish,
         out_shape=(

time: 79.8 us -> 77.3 us (0.969)
  local copies, waits for them, and re-layouts: 1.94 us -> 0 us
    unnamed x4 -> x0, local copies, waits for them, and re-layouts: 1.94 us -> none
where the time goes in v4:
time: 77.3 us; the launch traced here: 77.2 us
  Pallas kernels  76.5 us (99%)
    pallas_call x1, Pallas kernels, body(): pl.pallas_call(kernel, out_shape=(jax.ShapeDtypeStruct((R, D), BF16), jax...  75.1 us

profile of v4, /device:TPU:1, one launch (start us, length us, event | category | flops | bytes accessed | tf_op | source)
XLA Modules:
  0.0 77.2 jit_solution(17508707267482097713)
XLA Ops:
  0.6 75.1 %fused.1 = (bf16[192,1024]{1,0:T(8,128)(2,1)S(1)}, bf16[192,4096]{1,0:T(8,128)(2,1)S(1)}, bf16[128,1024]{1,0:T(8,128)(2,1)S(1)}) custom-call(bf16[192,4096]{1,0:T(8,128)(2,1)} %pre_ref.1, bf16[192,1024]{1,0:T(8,128)(2,1)} %og_ref.1, bf16[128,1024]{1,0:T(8,128)(2,1)} %w_ref.1), custom_call_target="tpu_custom_call" | custom-call | flops 4831838208 | bytes 4194304 | tf_op jit(solution)/shard_map/fused/pallas_call | solution.py:526
  75.7 1.5 %finish.1 = (bf16[192,1024]{1,0:T(8,128)(2,1)}, bf16[192,4096]{1,0:T(8,128)(2,1)}, f32[128,1024]{1,0:T(8,128)}) custom-call(bf16[192,1024]{1,0:T(8,128)(2,1)S(1)} %get-tuple-element.6.bo_ref, bf16[192,4096]{1,0:T(8,128)(2,1)S(1)} %get-tuple-element.7.pg_ref, bf16[128,1024]{1,0:T(8,128)(2,1)S(1)} %get-tuple-element.8.fo_ref), custom_call_target="tpu_custom_call" | custom-call | flops 131072 | bytes 3145728 | tf_op jit(solution)/shard_map/finish/pallas_call | solution.py:569
